TPU v7x, 32 devices: a whole 2x2x4 slice. The times are simulated.
32 devices in a mesh: fibre: 16 (over z, x, core), freq: 2 (over y).
Axes of the slice: x: 2, y: 2, z: 4, core: 2. Of those that a mesh axis runs over, the one named last changes fastest.
Arguments:
- traces: bfloat16 [2, 1024, 4096], P(None, 'fibre'), may hold values from -50 to 50, as said below
- live: int32 [1024], P('fibre'), may hold values 0 or 1
- reach: int32 [16], P('fibre'), may hold values from 1 to 8
Outputs:
- correlations: float32 [16, 8, 64, 64, 128], P('fibre', 'freq')
Inputs may be any that keep to these rules, and one draw needn't show every extreme that they name: `traces`: records of the fibre's channels.
All inputs are finite; a program needn't handle non-finite values. No bound on the sum of `live` on one device may be relied on, other than what follows from the above.
Results may differ from a plain program's by a relative error of at most 0.0057.
Values may be sent and summed in bfloat16 or wider, within the bound.
No kernel may reach another device: no remote copies, remote signals or barrier semaphores. Data moves between devices by JAX's collectives and lax.ppermute only.
A program may use at most 64 MiB of HBM per device.

v0:
```python
import functools
import math

import jax
import jax.numpy as jnp
import ml_dtypes
import numpy as np
from jax import lax
from jax.experimental import pallas as pl
from jax.experimental.pallas import tpu as pltpu
from jax.sharding import PartitionSpec as P

BAND = 64
OFF = 8
LAGS = 128


def leak_spectrum(freqs, samples, window, shift, slots, period):
    steps = np.arange(window)
    tone = np.exp(2j * np.pi * ((freqs[:, None] * (steps - shift)[None]) % samples) / samples)
    bins = np.exp(-2j * np.pi * ((steps[:, None] * slots[None]) % period) / period)
    return tone @ bins


@functools.lru_cache(maxsize=None)
def build_tables(samples):
    width = LAGS
    residues = samples // width
    groups = residues // 2
    half = width // 2
    per_band = BAND // residues
    order = np.concatenate([np.arange(i, half, per_band) for i in range(per_band)])
    steps = np.arange(width)
    slots = np.arange(width + 1)
    forward = np.zeros((groups, 2 * width, 4 * half))
    to_bins = np.zeros((2, groups, 4 * half, 4, width))
    root = 1.0 / math.sqrt(2.0)
    re_a, im_a, re_b, im_b = (slice(i * half, (i + 1) * half) for i in range(4))
    for g in range(groups):
        freq_a = g + residues * order
        freq_b = (residues - g if g else groups) + residues * order
        wave_a = np.exp(-2j * np.pi * ((steps[:, None] * freq_a[None]) % samples) / samples)
        wave_b = np.exp(-2j * np.pi * ((steps[:, None] * freq_b[None]) % samples) / samples)
        top, low = forward[g, :width], forward[g, width:]
        top[:, re_a], top[:, im_a] = wave_a.real, wave_a.imag
        if g == 0:
            low[:, re_b], low[:, im_b] = wave_b.real, wave_b.imag
        else:
            low[:, re_a], low[:, im_a] = -wave_a.imag, wave_a.real
            top[:, re_b], top[:, im_b] = wave_b.real, wave_b.imag
            low[:, re_b], low[:, im_b] = wave_b.imag, -wave_b.real
        for side in range(2):
            window, shift = ((width, 0), (2 * width, half))[side]
            leak = functools.partial(
                leak_spectrum, samples=samples, window=window, shift=shift, slots=slots, period=2 * width
            )
            pos_a, neg_a, pos_b, neg_b = leak(freq_a), leak(-freq_a), leak(freq_b), leak(-freq_b)
            spec = np.zeros((2, 4 * half, width + 1), complex)
            if g == 0:
                zero = (freq_a == 0)[:, None]
                spec[0, re_a] = np.where(zero, pos_a, root * (pos_a + neg_a))
                spec[0, im_a] = np.where(zero, 0.0, root * 1j * (pos_a - neg_a))
                spec[1, re_b] = root * (pos_b + neg_b)
                spec[1, im_b] = root * 1j * (pos_b - neg_b)
            else:
                spec[0, re_a], spec[0, im_a] = root * pos_a, root * 1j * pos_a
                spec[0, re_b], spec[0, im_b] = root * neg_b, -root * 1j * neg_b
                spec[1, re_b], spec[1, im_b] = root * pos_b, root * 1j * pos_b
                spec[1, re_a], spec[1, im_a] = root * neg_a, -root * 1j * neg_a
            table = to_bins[side, g]
            table[:, 0], table[:, 1] = spec[0, :, :width].real, spec[0, :, :width].imag
            table[:, 2], table[:, 3] = spec[1, :, :width].real, spec[1, :, :width].imag
            if g == 0:
                ends = (spec[0, :, 0].real, spec[1, :, 0].real, spec[0, :, width].real, spec[1, :, width].real)
            else:
                ends = tuple(
                    math.sqrt(2.0) * v
                    for v in (spec[0, :, 0].real, spec[0, :, 0].imag, spec[0, :, width].real, spec[0, :, width].imag)
                )
            for q in range(4):
                table[:, q, 0] = ends[q]
    lags = np.arange(LAGS)
    phase = 2 * np.pi * ((steps[:, None] * lags[None]) % (2 * width)) / (2 * width)
    lag = np.stack([2 * np.cos(phase), -2 * np.sin(phase)])
    lag[0, 0], lag[1, 0] = 1.0, (-1.0) ** lags
    bf16 = ml_dtypes.bfloat16
    forward_t = forward.transpose(0, 2, 1)
    forward_hi = forward_t.astype(bf16)
    forward_lo = (forward_t - forward_hi.astype(np.float64)).astype(bf16)
    bins_t = to_bins.transpose(0, 1, 3, 4, 2).reshape(2, groups, 4 * width, 4 * half).astype(bf16)
    lag = lag.reshape(2 * width, LAGS).T.astype(bf16)
    scale = residues / (2.0 * width * samples) / math.sqrt(samples)
    return forward_hi, forward_lo, bins_t, lag, scale


def real_dft(values):
    n = len(values)
    if n == 2:
        return [(values[0] + values[1], None), (values[0] - values[1], None)]
    even, odd = real_dft(values[0::2]), real_dft(values[1::2])
    out = [None] * (n // 2 + 1)
    for k in range(n // 4 + 1):
        (er, ei), (pr, pi) = even[k], odd[k]
        angle = -2.0 * math.pi * k / n
        c, s = math.cos(angle), math.sin(angle)
        if k == 0:
            out[0] = (er + pr, None)
            out[n // 2] = (er - pr, None)
            continue
        if 4 * k == n:
            out[k] = (er, -pr)
            continue
        if pi is None:
            tr, ti = pr * c, pr * s
        elif 8 * k == n:
            tr, ti = (pr + pi) * c, (pi - pr) * c
        else:
            tr, ti = pr * c - pi * s, pr * s + pi * c
        if ei is None:
            out[k] = (er + tr, ti)
            out[n // 2 - k] = (er - tr, ti)
        else:
            out[k] = (er + tr, ei + ti)
            out[n // 2 - k] = (er - tr, ti - ei)
    return out


def whiten(copies_of, records, copies, fhi, flo, yhi, ylo, spec):
    channels, samples = records[0].shape
    width = LAGS
    residues = samples // width
    groups = residues // 2
    rows = len(records) * copies_of * channels
    tiles = rows // width
    step = 16

    def split(value):
        high = value.astype(jnp.bfloat16)
        return high, (value - high.astype(jnp.float32)).astype(jnp.bfloat16)

    def transform(n, carry):
        for index, ref in enumerate(records):
            block = ref[pl.ds(pl.multiple_of(n * step, step), step), :].astype(jnp.float32)
            terms = real_dft([block[:, a * width:(a + 1) * width] for a in range(residues)])
            for g in range(groups):
                parts = terms[g] if g else (terms[0][0], terms[groups][0])
                for side, part in enumerate(parts):
                    hi, lo = split(part)
                    for copy_to in range(copies_of):
                        row = pl.multiple_of((index * copies_of + copy_to) * channels + n * step, step)
                        yhi[g, pl.ds(row, step), side * width:(side + 1) * width] = hi
                        ylo[g, pl.ds(row, step), side * width:(side + 1) * width] = lo
        return carry

    lax.fori_loop(0, channels // step, transform, 0)
    copies[0].wait()
    copies[1].wait()
    nt = (((1,), (1,)), ((), ()))
    bands = (samples // 2) // BAND

    def place(g, tile):
        return pl.ds(pl.multiple_of((g * tiles + tile) * 2 * width, 2 * width), 2 * width)

    def forward(g, power):
        value = lax.dot_general(fhi[g], yhi[g], nt, preferred_element_type=jnp.float32)
        value += lax.dot_general(flo[g], yhi[g], nt, preferred_element_type=jnp.float32)
        value += lax.dot_general(fhi[g], ylo[g], nt, preferred_element_type=jnp.float32)
        for tile in range(tiles):
            spec[place(g, tile), :] = value[:, tile * width:(tile + 1) * width]
        squared = (value * value).reshape(2 * width // bands, bands, rows)
        return power + squared.sum(0)

    power = lax.fori_loop(0, groups, forward, jnp.zeros((bands, rows), jnp.float32), unroll=8)
    gain = 1.0 / jnp.sqrt(power * (1.0 / BAND) + 1e-6)

    def white(g):
        value = jnp.concatenate([spec[place(g, tile), :] for tile in range(tiles)], axis=1)
        value = value.reshape(2 * width // bands, bands, rows) * gain[None]
        return value.reshape(2 * width, rows).astype(jnp.bfloat16)

    return white


def start_copies(sources, targets, sems):
    copies = [
        pltpu.make_async_copy(source, target, sems.at[i])
        for i, (source, target) in enumerate(zip(sources, targets))
    ]
    for copy in copies:
        copy.start()
    return copies


def write_out(chunks, fill, stage, out_hbm, sems):
    per_chunk = stage.shape[0] // chunks
    copies = []
    for chunk in range(chunks):
        def one(n, carry):
            stage[chunk * per_chunk + n] = fill(chunk * per_chunk + n)
            return carry

        lax.fori_loop(0, per_chunk, one, 0, unroll=8)
        part = pl.ds(chunk * per_chunk, per_chunk)
        copies.append(pltpu.make_async_copy(stage.at[part], out_hbm.at[part], sems.at[chunk]))
        copies[-1].start()
    for copy in copies:
        copy.wait()


def own_spectra_kernel(windows, *refs):
    records, (fhi_hbm, flo_hbm, out_ref, fhi, flo, yhi, ylo, spec, sems) = refs[:windows], refs[windows:]
    copies = start_copies((fhi_hbm, flo_hbm), (fhi, flo), sems)
    white = whiten(2, records, copies, fhi, flo, yhi, ylo, spec)

    def write(g, carry):
        out_ref[g] = white(g)
        return carry

    lax.fori_loop(0, out_ref.shape[0], write, 0, unroll=4)


def own_bins_kernel(windows, white_ref, bins_hbm, out_hbm, bins, wide, stage, sems, out_sems):
    groups, rows, _ = bins.shape
    width, lanes, depth = stage.shape
    chunks = sems.shape[0]
    per_chunk = groups // chunks
    parts = [pl.ds(chunk * per_chunk, per_chunk) for chunk in range(chunks)]
    copies = start_copies([bins_hbm.at[p] for p in parts], [bins.at[p] for p in parts], sems)
    left = lax.broadcasted_iota(jnp.int32, (width, windows * lanes), 1) % lanes < lanes // 2
    ends = lax.broadcasted_iota(jnp.int32, (width, windows * lanes), 0) == 0
    for chunk in range(chunks):
        copies[chunk].wait()
        for g in range(chunk * per_chunk, (chunk + 1) * per_chunk):
            value = jnp.dot(bins[g], white_ref[g], preferred_element_type=jnp.float32)
            parts = [value[q * width:(q + 1) * width] for q in range(4)]
            turned = [parts[1], -parts[0], parts[3], -parts[2]]
            zero = jnp.zeros_like(parts[0])
            for q in range(4):
                real = parts[q] if q < 2 else jnp.where(ends, zero, parts[q])
                imag = jnp.where(ends, zero if q < 2 else parts[q], turned[q])
                both = jnp.where(left, real, imag)
                for w in range(windows):
                    start = w * (groups * 4) + g * 4 + q
                    wide[pl.ds(start, width, stride=depth + 1), :] = both[:, w * lanes:(w + 1) * lanes]

    def turn(k):
        return wide[pl.ds(k * (depth + 1), depth), :].T.astype(jnp.bfloat16)

    write_out(out_sems.shape[0], turn, stage, out_hbm, out_sems)


def fill_bins(white, bins, wide):
    groups, rows, _ = bins.shape
    width = rows // 4

    def to_bins(g, carry):
        value = jnp.dot(bins[g], white(g), preferred_element_type=jnp.float32)
        for q in range(4):
            for tile, ref in enumerate(wide):
                ref[pl.ds(g * 4 + q, width, stride=groups * 4 + 1), :] = (
                    value[q * width:(q + 1) * width, tile * width:(tile + 1) * width]
                )
        return carry

    lax.fori_loop(0, groups, to_bins, 0, unroll=8)


def partner_bins(wide, k, depth):
    part = pl.ds(k * (depth + 1), depth)
    return jnp.concatenate([ref[part, :].astype(jnp.bfloat16) for ref in wide], axis=0)


def pair_kernel(windows, *refs):
    records, sources, refs = refs[:2 * windows], refs[2 * windows:2 * windows + 3], refs[2 * windows + 3:]
    out_hbm, fhi, flo, bins, yhi, ylo, spec, *wide, stage, sems, out_sems = refs
    copies = start_copies(sources, (fhi, flo, bins), sems)
    white = whiten(1, records, copies, fhi, flo, yhi, ylo, spec)
    copies[2].wait()
    fill_bins(white, bins, wide)
    depth = stage.shape[1] // windows
    write_out(out_sems.shape[0], lambda k: partner_bins(wide, k, depth), stage, out_hbm, out_sems)


def last_kernel(windows, earlier, *refs):
    records, refs = refs[:2 * windows], refs[2 * windows:]
    count, pairs = 4 + earlier, 1 + earlier
    sources, (lag_ref, slot_ref, keep_ref, out_hbm), scratch = refs[:count], refs[count:count + 4], refs[count + 4:]
    loaded, (yhi, ylo, *scratch) = scratch[:count], scratch[count:]
    wide, cross, (stage, sems, out_sems) = scratch[:windows], scratch[windows:windows + pairs], scratch[windows + pairs:]
    fhi, flo, bins, own_ref, *early = loaded
    copies = start_copies(sources, loaded, sems)
    white = whiten(1, records, copies, fhi, flo, yhi, ylo, cross[0])
    copies[2].wait()
    fill_bins(white, bins, wide)
    for copy in copies[3:]:
        copy.wait()
    width, lanes, _ = own_ref.shape
    channels = lanes // 2
    depth = bins.shape[0] * 4

    def one_bin(k, carry):
        block = jnp.concatenate([ref[k] for ref in early] + [partner_bins(wide, k, depth)], axis=1)
        value = jnp.dot(own_ref[k], block, preferred_element_type=jnp.float32)
        for tile, ref in enumerate(cross):
            for part in range(2):
                ref[pl.ds(part * width + k, channels, stride=2 * width + 1), :] = (
                    value[part * channels:(part + 1) * channels, tile * lanes:(tile + 1) * lanes]
                )
        return carry

    lax.fori_loop(0, width, one_bin, 0, unroll=16)
    rows = 2 * width
    _, offsets, per_out, channels, _ = stage.shape
    chunks = channels // per_out

    def leave(chunk, slot):
        target = out_hbm.at[:, pl.ds(chunk * per_out, per_out)]
        return pltpu.make_async_copy(stage.at[slot], target, out_sems.at[slot])

    def two_chunks(t, carry):
        for slot in range(2):
            chunk = t * 2 + slot

            @pl.when(t > 0)
            def _():
                leave(chunk - 2, slot).wait()

            def one(n, inner):
                i = chunk * per_out + n
                block = jnp.concatenate(
                    [ref[pl.ds(i * (rows + 1), rows), :].astype(jnp.bfloat16) for ref in cross], axis=1
                )
                value = jnp.dot(lag_ref[...], block, preferred_element_type=jnp.float32).T
                for o in range(offsets):
                    stage[slot, slot_ref[o], n] = value[o * channels:(o + 1) * channels] * keep_ref[o]
                return inner

            lax.fori_loop(0, per_out, one, 0, unroll=8)
            leave(chunk, slot).start()
        return carry

    lax.fori_loop(0, chunks // 2, two_chunks, 0)
    for slot in range(2):
        leave(chunks - 2 + slot, slot).wait()


def call(kernel, name, operands, streamed, small, out_shape, out_space, scratch, flops, limit=50):
    vmem_spec = pl.BlockSpec(memory_space=pltpu.VMEM)
    smem_spec = pl.BlockSpec(memory_space=pltpu.SMEM)
    return pl.pallas_call(
        kernel,
        out_shape=out_shape,
        in_specs=[vmem_spec] * len(operands)
        + [pl.BlockSpec(memory_space=pl.ANY)] * len(streamed)
        + [vmem_spec if v.ndim > 1 else smem_spec for v in small],
        out_specs=pl.BlockSpec(memory_space=out_space),
        scratch_shapes=scratch,
        compiler_params=pltpu.CompilerParams(vmem_limit_bytes=limit * 2**20),
        cost_estimate=pl.CostEstimate(flops=flops, bytes_accessed=14 * 2**20, transcendentals=0),
        name=name,
    )(*operands, *streamed, *small)


def per_device(traces, live, reach):
    windows, channels, samples = traces.shape
    blocks = lax.axis_size("fibre")
    splits = lax.axis_size("freq")
    owned = OFF // splits
    place = lax.axis_index("freq")
    forward_hi, forward_lo, bins_t, lag, scale = build_tables(samples)
    forward_hi, forward_lo = jnp.asarray(forward_hi), jnp.asarray(forward_lo)
    masked = [jnp.where(live[:, None] > 0, traces[w], jnp.zeros((), traces.dtype)) for w in range(windows)]

    quads = blocks // owned
    half = owned // 2
    u = lax.axis_index("fibre") % owned
    core, pair = u % half, u // half

    def rank(q, pair, core, part):
        return (q * owned + pair * half + core) * splits + part

    def send(payload, route):
        pairs = []
        for q in range(quads):
            for p in range(2):
                for c in range(half):
                    for g in range(splits):
                        source = route(q, p, c, g)
                        if source[0] < quads:
                            pairs.append((rank(*source), rank(q, p, c, g)))
        return lax.ppermute(payload, ("fibre", "freq"), pairs)

    def from_neighbours(mine, upper):
        core_payload = jnp.where((core == 1) & (place == 0), mine, upper)
        across_payload = jnp.where((pair == 1) & (place == 0), mine, upper)
        beside = send(core_payload, lambda q, p, c, g: (q + c * g, p, 1 - c, 1 - g if c else g))
        across = send(across_payload, lambda q, p, c, g: (q + p * g, 1 - p, c, g))
        return jnp.where(place == 0, mine, upper), beside, across

    width = LAGS
    lanes = 2 * channels
    groups = samples // width // 2
    depth = 4 * groups
    pairs = 2
    bf16, f32 = jnp.bfloat16, jnp.float32
    dma = pltpu.SemaphoreType.DMA
    table_shapes = [pltpu.VMEM(t.shape, bf16) for t in (forward_hi, forward_lo, bins_t[0])]
    own_table, partner_table = jnp.asarray(bins_t[1]), jnp.asarray(bins_t[0])
    split_shapes = [pltpu.VMEM((groups, 2 * lanes, 2 * width), bf16)] * 2
    spec_shape = pltpu.VMEM((groups * 2 * lanes // width * 2 * width, width), f32)
    wide_shapes = [pltpu.VMEM((width * (depth + 1), lanes), f32)] * windows
    work = 16 * groups * 2 * lanes * 4 * width * width

    above = lambda q, p, c, g: (quads if p and c and not g else q + 1, p, c, g)
    upper = [send(mine, above) for mine in masked]
    own_white = call(
        functools.partial(own_spectra_kernel, windows), "own_spectra", masked, (forward_hi, forward_lo), (),
        jax.ShapeDtypeStruct((groups, 2 * width, windows * lanes), bf16), pltpu.VMEM,
        table_shapes[:2] + split_shapes + [spec_shape, dma((2,))], work // 2,
    )
    upper[0], own_white = lax.optimization_barrier((upper[0], own_white))
    own_shape = (width, lanes, windows * depth)
    own = call(
        functools.partial(own_bins_kernel, windows), "own_bins", [own_white], [own_table], (),
        jax.ShapeDtypeStruct(own_shape, bf16), pl.ANY,
        [table_shapes[2], pltpu.VMEM((width * (windows * depth + 1), lanes), f32), pltpu.VMEM(own_shape, bf16),
         dma((4,)), dma((4,))], work // 2,
    )
    here, beside, across = [], [], []
    for w in range(windows):
        if w:
            upper[w], beside[w - 1], own = lax.optimization_barrier((upper[w], beside[w - 1], own))
        for known, new in zip((here, beside, across), from_neighbours(masked[w], upper[w])):
            known.append(new)
    across[0], beside[-1] = lax.optimization_barrier((across[0], beside[-1]))
    shape = (width, windows * depth, lanes)
    first = call(
        functools.partial(pair_kernel, windows), "first_pair", [r for both in zip(here, beside) for r in both],
        (forward_hi, forward_lo, partner_table), (), jax.ShapeDtypeStruct(shape, bf16), pl.ANY,
        table_shapes + split_shapes + [spec_shape] + wide_shapes
        + [pltpu.VMEM(shape, bf16), dma((3,)), dma((4,))], work,
    )
    across[-1], first = lax.optimization_barrier((across[-1], first))
    across_beside = [send(block, lambda q, p, c, g: (q, p, 1 - c, g)) for block in across]
    early = [first]
    slots = jnp.stack([0, 1 + 2 * core, 2, 3 - 2 * core]).astype(jnp.int32)
    offset_ids = place * owned + slots
    keep = jnp.where(offset_ids < reach[0], jnp.float32(scale), jnp.float32(0.0))
    result = call(
        functools.partial(last_kernel, windows, len(early)), "second_pair",
        [r for both in zip(across, across_beside) for r in both],
        (forward_hi, forward_lo, partner_table, own, *early), (jnp.asarray(lag), slots, keep),
        jax.ShapeDtypeStruct((owned, channels, channels, LAGS), f32), pl.ANY,
        table_shapes + [pltpu.VMEM(own_shape, bf16)] + [pltpu.VMEM(e.shape, bf16) for e in early]
        + split_shapes + wide_shapes + [pltpu.VMEM((channels * (2 * width + 1), lanes), f32)] * pairs
        + [pltpu.VMEM((2, owned, channels // 8, channels, LAGS), f32), dma((4 + len(early),)), dma((2,))],
        2 * work,
    )
    return result[None]


def solution(mesh):
    placed = (P(None, "fibre", None), P("fibre"), P("fibre"))
    return jax.shard_map(
        per_device,
        mesh=mesh,
        in_specs=placed,
        out_specs=P("fibre", "freq", None, None, None),
        check_vma=False,
    )
```

profile of v0, /device:TPU:21, one launch (start us, length us, event | category | flops | bytes accessed | tf_op | source)
XLA Modules:
  0.0 72.3 jit_solution(16344032418354500054)
XLA Ops:
  0.0 0.7 broadcast_compare_fusion
  0.7 1.3 %bitcast_select_fusion = (bf16[64,4096]{1,0:T(8,128)(2,1)S(1)}, bf16[64,4096]{1,0:T(8,128)(2,1)S(1)}) fusion(bf16[2,64,4096]{2,1,0:T(8,128)(2,1)} %param.8, pred[64]{0:T(512)(128)(4,1)S(1)} %broadcast_compare_fusion), kind=kLoop, calls=%fused_computation | loop fusion | flops 524288 | bytes 2097216 | tf_op jit(solution)/shard_map/jit(_where)/select_n | solution.py:372
  2.0 2.1 %collective-permute-start = (bf16[64,4096]{1,0:T(8,128)(2,1)S(1)}, bf16[64,4096]{1,0:T(8,128)(2,1)S(1)}, u32[]{:S(2)}, u32[]{:S(2)}) collective-permute-start(bf16[64,4096]{1,0:T(8,128)(2,1)S(1)} %get-tuple-element.26.refs_0_), channel_id=1, source_target_pairs={{8,0},{9,1},{10,2},{11,3},{12,4},{13,5},{15,7},{16,8},{17,9},{18,1... | collective-permute-start | bytes 1572872 | tf_op jit(solution)/shard_map/ppermute | solution.py:391
  4.1 2.1 %collective-permute-start.2 = (bf16[64,4096]{1,0:T(8,128)(2,1)S(1)}, bf16[64,4096]{1,0:T(8,128)(2,1)S(1)}, u32[]{:S(2)}, u32[]{:S(2)}) collective-permute-start(bf16[64,4096]{1,0:T(8,128)(2,1)S(1)} %get-tuple-element.25.refs_1_), channel_id=1, source_target_pairs={{8,0},{9,1},{10,2},{11,3},{12,4},{13,5},{15,7},{16,8},{17,9},{18,1... | collective-permute-start | bytes 1572872 | tf_op jit(solution)/shard_map/ppermute | solution.py:391
  6.2 4.5 %own_spectra.1.white_ref = bf16[16,256,256]{2,1,0:T(8,128)(2,1)S(1)} custom-call(bf16[64,4096]{1,0:T(8,128)(2,1)S(1)} %get-tuple-element.26.refs_0_, bf16[64,4096]{1,0:T(8,128)(2,1)S(1)} %get-tuple-element.25.refs_1_, bf16[16,256,256]{2,1,0:T(8,128)(2,1)} %constant.66.clone.refs_2_.refs_4_, bf16[16,256,256]{2,1,0:T(8,128)(2,1)} %constant.67.clone.refs_3_.refs_5_), custom_call_target="tpu_custom_call" | custom-call | flops 2147483648 | bytes 14680064 | tf_op jit(solution)/shard_map/own_spectra/pallas_call | solution.py:350
  10.8 5.9 %collective-permute-done = bf16[64,4096]{1,0:T(8,128)(2,1)S(1)} collective-permute-done((bf16[64,4096]{1,0:T(8,128)(2,1)S(1)}, bf16[64,4096]{1,0:T(8,128)(2,1)S(1)}, u32[]{:S(2)}, u32[]{:S(2)}) %collective-permute-start) | collective-permute-done | bytes 524320 | tf_op jit(solution)/shard_map/ppermute | solution.py:391
  16.7 0.1 broadcast_select_fusion.1
  16.8 4.6 %collective-permute-start.3 = (bf16[64,4096]{1,0:T(8,128)(2,1)S(1)}, bf16[64,4096]{1,0:T(8,128)(2,1)S(1)}, u32[]{:S(2)}, u32[]{:S(2)}) collective-permute-start(bf16[64,4096]{1,0:T(8,128)(2,1)S(1)} %get-tuple-element.31), channel_id=1, source_target_pairs={{2,0},{3,1},{1,2},{8,3},{6,4},{7,5},{5,6},{12,7},{10,8},{11,9},{9,... | collective-permute-start | bytes 1572872 | tf_op jit(solution)/shard_map/ppermute | solution.py:391
  21.4 3.0 %collective-permute-start.1 = (bf16[64,4096]{1,0:T(8,128)(2,1)S(1)}, bf16[64,4096]{1,0:T(8,128)(2,1)S(1)}, u32[]{:S(2)}, u32[]{:S(2)}) collective-permute-start(bf16[64,4096]{1,0:T(8,128)(2,1)S(1)} %get-tuple-element.32), channel_id=1, source_target_pairs={{4,0},{5,1},{6,2},{7,3},{0,4},{9,5},{2,6},{11,7},{12,8},{13,9},{14... | collective-permute-start | bytes 1572872 | tf_op jit(solution)/shard_map/ppermute | solution.py:391
  24.4 6.4 %own_bins.1.refs_7_ = bf16[128,128,128]{2,1,0:T(8,128)(2,1)} custom-call(bf16[16,256,256]{2,1,0:T(8,128)(2,1)S(1)} %own_spectra.1.white_ref, bf16[16,512,256]{2,1,0:T(8,128)(2,1)} %constant.68.clone.bins_hbm), custom_call_target="tpu_custom_call" | custom-call | flops 2147483648 | bytes 14680064 | tf_op jit(solution)/shard_map/own_bins/pallas_call | solution.py:350
  30.8 0.0 collective-permute-done.2
  30.8 3.5 %collective-permute-done.3.refs_1_ = bf16[64,4096]{1,0:T(8,128)(2,1)S(1)} collective-permute-done((bf16[64,4096]{1,0:T(8,128)(2,1)S(1)}, bf16[64,4096]{1,0:T(8,128)(2,1)S(1)}, u32[]{:S(2)}, u32[]{:S(2)}) %collective-permute-start.3) | collective-permute-done | bytes 524320 | tf_op jit(solution)/shard_map/ppermute | solution.py:391
  34.3 0.1 broadcast_select_fusion
  34.5 1.9 %collective-permute-start.4 = (bf16[64,4096]{1,0:T(8,128)(2,1)S(1)}, bf16[64,4096]{1,0:T(8,128)(2,1)S(1)}, u32[]{:S(2)}, u32[]{:S(2)}) collective-permute-start(bf16[64,4096]{1,0:T(8,128)(2,1)S(1)} %get-tuple-element.29), channel_id=1, source_target_pairs={{2,0},{3,1},{1,2},{8,3},{6,4},{7,5},{5,6},{12,7},{10,8},{11,9},{9,... | collective-permute-start | bytes 1572872 | tf_op jit(solution)/shard_map/ppermute | solution.py:391
  36.4 1.9 %collective-permute-start.6 = (bf16[64,4096]{1,0:T(8,128)(2,1)S(1)}, bf16[64,4096]{1,0:T(8,128)(2,1)S(1)}, u32[]{:S(2)}, u32[]{:S(2)}) collective-permute-start(bf16[64,4096]{1,0:T(8,128)(2,1)S(1)} %get-tuple-element.28), channel_id=1, source_target_pairs={{4,0},{5,1},{6,2},{7,3},{0,4},{9,5},{2,6},{11,7},{12,8},{13,9},{14... | collective-permute-start | bytes 1572872 | tf_op jit(solution)/shard_map/ppermute | solution.py:391
  38.3 0.0 collective-permute-done.1.refs_0_
  38.3 7.5 %collective-permute-done.4.refs_3_ = bf16[64,4096]{1,0:T(8,128)(2,1)S(1)} collective-permute-done((bf16[64,4096]{1,0:T(8,128)(2,1)S(1)}, bf16[64,4096]{1,0:T(8,128)(2,1)S(1)}, u32[]{:S(2)}, u32[]{:S(2)}) %collective-permute-start.4) | collective-permute-done | bytes 524320 | tf_op jit(solution)/shard_map/ppermute | solution.py:391
  45.9 0.0 collective-permute-start.5
  45.9 0.0 copy-start
  45.9 7.9 %first_pair.1.refs_8_ = bf16[128,128,128]{2,1,0:T(8,128)(2,1)} custom-call(bf16[64,4096]{1,0:T(8,128)(2,1)S(1)} %get-tuple-element.30.refs_0_, bf16[64,4096]{1,0:T(8,128)(2,1)S(1)} %collective-permute-done.3.refs_1_, bf16[64,4096]{1,0:T(8,128)(2,1)S(1)} %get-tuple-element.27.refs_2_, bf16[64,4096]{1,0:T(8,128)(2,1)S(1)} %collective-permute-done.4.refs_3_, ...), custom_call_target="tpu_custom_call" | custom-call | flops 4294967296 | bytes 14680064 | tf_op jit(solution)/shard_map/first_pair/pallas_call | solution.py:350
  53.7 0.0 collective-permute-done.6.refs_2_
  53.7 0.6 collective-permute-start.7
  55.0 0.1 compare_select_fusion
  55.1 0.0 collective-permute-done.5.refs_1_
  55.1 0.8 %collective-permute-done.7.refs_3_ = bf16[64,4096]{1,0:T(8,128)(2,1)S(1)} collective-permute-done((bf16[64,4096]{1,0:T(8,128)(2,1)S(1)}, bf16[64,4096]{1,0:T(8,128)(2,1)S(1)}, u32[]{:S(2)}, u32[]{:S(2)}) %collective-permute-start.7) | collective-permute-done | bytes 524320 | tf_op jit(solution)/shard_map/ppermute | solution.py:391
  55.9 0.0 copy-done
  55.9 16.4 %second_pair.1 = f32[4,64,64,128]{3,2,1,0:T(8,128)} custom-call(bf16[64,4096]{1,0:T(8,128)(2,1)S(1)} %collective-permute-done.1.refs_0_, bf16[64,4096]{1,0:T(8,128)(2,1)S(1)} %collective-permute-done.5.refs_1_, bf16[64,4096]{1,0:T(8,128)(2,1)S(1)} %collective-permute-done.6.refs_2_, bf16[64,4096]{1,0:T(8,128)(2,1)S(1)} %collective-permute-done.7.refs_3_, ...), custom_call_target="tpu_custom_call" | custom-call | flops 8589934592 | bytes 14680064 | tf_op jit(solution)/shard_map/second_pair/pallas_call | solution.py:350
Async XLA Ops:
  2.0 14.7 %collective-permute-start = (bf16[64,4096]{1,0:T(8,128)(2,1)S(1)}, bf16[64,4096]{1,0:T(8,128)(2,1)S(1)}, u32[]{:S(2)}, u32[]{:S(2)}) collective-permute-start(bf16[64,4096]{1,0:T(8,128)(2,1)S(1)} %get-tuple-element.26.refs_0_), channel_id=1, source_target_pairs={{8,0},{9,1},{10,2},{11,3},{12,4},{13,5},{15,7},{16,8},{17,9},{18,1... | collective-permute-start | bytes 1572872 | tf_op jit(solution)/shard_map/ppermute | solution.py:391
  4.1 26.7 %collective-permute-start.2 = (bf16[64,4096]{1,0:T(8,128)(2,1)S(1)}, bf16[64,4096]{1,0:T(8,128)(2,1)S(1)}, u32[]{:S(2)}, u32[]{:S(2)}) collective-permute-start(bf16[64,4096]{1,0:T(8,128)(2,1)S(1)} %get-tuple-element.25.refs_1_), channel_id=1, source_target_pairs={{8,0},{9,1},{10,2},{11,3},{12,4},{13,5},{15,7},{16,8},{17,9},{18,1... | collective-permute-start | bytes 1572872 | tf_op jit(solution)/shard_map/ppermute | solution.py:391
  16.8 17.5 %collective-permute-start.3 = (bf16[64,4096]{1,0:T(8,128)(2,1)S(1)}, bf16[64,4096]{1,0:T(8,128)(2,1)S(1)}, u32[]{:S(2)}, u32[]{:S(2)}) collective-permute-start(bf16[64,4096]{1,0:T(8,128)(2,1)S(1)} %get-tuple-element.31), channel_id=1, source_target_pairs={{2,0},{3,1},{1,2},{8,3},{6,4},{7,5},{5,6},{12,7},{10,8},{11,9},{9,... | collective-permute-start | bytes 1572872 | tf_op jit(solution)/shard_map/ppermute | solution.py:391
  21.4 16.9 %collective-permute-start.1 = (bf16[64,4096]{1,0:T(8,128)(2,1)S(1)}, bf16[64,4096]{1,0:T(8,128)(2,1)S(1)}, u32[]{:S(2)}, u32[]{:S(2)}) collective-permute-start(bf16[64,4096]{1,0:T(8,128)(2,1)S(1)} %get-tuple-element.32), channel_id=1, source_target_pairs={{4,0},{5,1},{6,2},{7,3},{0,4},{9,5},{2,6},{11,7},{12,8},{13,9},{14... | collective-permute-start | bytes 1572872 | tf_op jit(solution)/shard_map/ppermute | solution.py:391
  34.5 11.4 %collective-permute-start.4 = (bf16[64,4096]{1,0:T(8,128)(2,1)S(1)}, bf16[64,4096]{1,0:T(8,128)(2,1)S(1)}, u32[]{:S(2)}, u32[]{:S(2)}) collective-permute-start(bf16[64,4096]{1,0:T(8,128)(2,1)S(1)} %get-tuple-element.29), channel_id=1, source_target_pairs={{2,0},{3,1},{1,2},{8,3},{6,4},{7,5},{5,6},{12,7},{10,8},{11,9},{9,... | collective-permute-start | bytes 1572872 | tf_op jit(solution)/shard_map/ppermute | solution.py:391
  36.4 17.4 %collective-permute-start.6 = (bf16[64,4096]{1,0:T(8,128)(2,1)S(1)}, bf16[64,4096]{1,0:T(8,128)(2,1)S(1)}, u32[]{:S(2)}, u32[]{:S(2)}) collective-permute-start(bf16[64,4096]{1,0:T(8,128)(2,1)S(1)} %get-tuple-element.28), channel_id=1, source_target_pairs={{4,0},{5,1},{6,2},{7,3},{0,4},{9,5},{2,6},{11,7},{12,8},{13,9},{14... | collective-permute-start | bytes 1572872 | tf_op jit(solution)/shard_map/ppermute | solution.py:391
  45.9 9.2 %collective-permute-start.5 = (bf16[64,4096]{1,0:T(8,128)(2,1)S(1)}, bf16[64,4096]{1,0:T(8,128)(2,1)S(1)}, u32[]{:S(2)}, u32[]{:S(2)}) collective-permute-start(bf16[64,4096]{1,0:T(8,128)(2,1)S(1)} %collective-permute-done.1.refs_0_), channel_id=1, source_target_pairs={{2,0},{3,1},{0,2},{1,3},{6,4},{7,5},{4,6},{5,7},{10,8},{11,9},{8,1... | collective-permute-start | bytes 1572872 | tf_op jit(solution)/shard_map/ppermute | solution.py:391
  45.9 10.0 %copy-start = (bf16[128,256]{1,0:T(8,128)(2,1)S(1)}, bf16[128,256]{1,0:T(8,128)(2,1)}, u32[]{:S(2)}) copy-start(bf16[128,256]{1,0:T(8,128)(2,1)} %constant.70.clone.refs_9_) | copy-start | bytes 196612
  53.7 2.1 %collective-permute-start.7 = (bf16[64,4096]{1,0:T(8,128)(2,1)S(1)}, bf16[64,4096]{1,0:T(8,128)(2,1)S(1)}, u32[]{:S(2)}, u32[]{:S(2)}) collective-permute-start(bf16[64,4096]{1,0:T(8,128)(2,1)S(1)} %collective-permute-done.6.refs_2_), channel_id=1, source_target_pairs={{2,0},{3,1},{0,2},{1,3},{6,4},{7,5},{4,6},{5,7},{10,8},{11,9},{8,1... | collective-permute-start | bytes 1572872 | tf_op jit(solution)/shard_map/ppermute | solution.py:391
where the time goes:
time: 72.6 us; the launch traced here: 72.3 us
  Pallas kernels  35.2 us (48%)
  waiting for transfers between devices  17.8 us (25%)
  starting transfers between devices  16.2 us (22%)
  other arithmetic  2.29 us (3%)
  between operations  0.82 us (1%)
    pallas_call x4, Pallas kernels, call(): pl.pallas_call(kernel, out_shape=out_shape, in_specs=[vmem_spec] * len(op...  35.2 us
    ppermute x8, waiting for transfers between devices, send(): return lax.ppermute(payload, ('fibre', 'freq'), pairs)  17.8 us
    ppermute x8, starting transfers between devices, send(): return lax.ppermute(payload, ('fibre', 'freq'), pairs)  16.2 us
  transfers between devices with their start and end apart: 8, of which 4 were waited for; matrix products, arithmetic and copies ran while one was open for 0% of the time, Pallas kernels for 26%

commit v1 on v0

--- a/solution.py
+++ b/solution.py
@@ -207,6 +207,17 @@
         copy.wait()
 
 
+def mask_kernel(traces_ref, live_ref, *out_refs):
+    channels = live_ref.shape[1]
+    square = (channels, channels)
+    same = lax.broadcasted_iota(jnp.int32, square, 0) == lax.broadcasted_iota(jnp.int32, square, 1)
+    live = jnp.broadcast_to((live_ref[...] > 0).astype(jnp.float32), square)
+    pick = jnp.where(same, live, 0.0).astype(jnp.bfloat16)
+    for w, out_ref in enumerate(out_refs):
+        value = jnp.dot(pick, traces_ref[w], preferred_element_type=jnp.float32)
+        out_ref[...] = value.astype(jnp.bfloat16)
+
+
 def own_spectra_kernel(windows, *refs):
     records, (fhi_hbm, flo_hbm, out_ref, fhi, flo, yhi, ylo, spec, sems) = refs[:windows], refs[windows:]
     copies = start_copies((fhi_hbm, flo_hbm), (fhi, flo), sems)
@@ -369,7 +380,14 @@
     place = lax.axis_index("freq")
     forward_hi, forward_lo, bins_t, lag, scale = build_tables(samples)
     forward_hi, forward_lo = jnp.asarray(forward_hi), jnp.asarray(forward_lo)
-    masked = [jnp.where(live[:, None] > 0, traces[w], jnp.zeros((), traces.dtype)) for w in range(windows)]
+    masked = list(pl.pallas_call(
+        mask_kernel,
+        out_shape=[jax.ShapeDtypeStruct((channels, samples), traces.dtype)] * windows,
+        in_specs=[pl.BlockSpec(memory_space=pltpu.VMEM)] * 2,
+        out_specs=[pl.BlockSpec(memory_space=pltpu.VMEM)] * windows,
+        compiler_params=pltpu.CompilerParams(vmem_limit_bytes=61 * 2**20),
+        name="mask_dead",
+    )(traces, live[None, :]))
 
     quads = blocks // owned
     half = owned // 2
@@ -390,12 +408,13 @@
                             pairs.append((rank(*source), rank(q, p, c, g)))
         return lax.ppermute(payload, ("fibre", "freq"), pairs)
 
-    def from_neighbours(mine, upper):
-        core_payload = jnp.where((core == 1) & (place == 0), mine, upper)
-        across_payload = jnp.where((pair == 1) & (place == 0), mine, upper)
-        beside = send(core_payload, lambda q, p, c, g: (q + c * g, p, 1 - c, 1 - g if c else g))
-        across = send(across_payload, lambda q, p, c, g: (q + p * g, 1 - p, c, g))
-        return jnp.where(place == 0, mine, upper), beside, across
+    def to_core(mine, upper):
+        payload = jnp.where((core == 1) & (place == 0), mine, upper)
+        return send(payload, lambda q, p, c, g: (q + c * g, p, 1 - c, 1 - g if c else g))
+
+    def to_pair(mine, upper):
+        payload = jnp.where((pair == 1) & (place == 0), mine, upper)
+        return send(payload, lambda q, p, c, g: (q + p * g, 1 - p, c, g))
 
     width = LAGS
     lanes = 2 * channels
@@ -426,12 +445,18 @@
         [table_shapes[2], pltpu.VMEM((width * (windows * depth + 1), lanes), f32), pltpu.VMEM(own_shape, bf16),
          dma((4,)), dma((4,))], work // 2,
     )
+    slots = jnp.stack([0, 1 + 2 * core, 2, 3 - 2 * core]).astype(jnp.int32)
+    offset_ids = place * owned + slots
+    keep = jnp.where(offset_ids < reach[0], jnp.float32(scale), jnp.float32(0.0))
     here, beside, across = [], [], []
     for w in range(windows):
         if w:
-            upper[w], beside[w - 1], own = lax.optimization_barrier((upper[w], beside[w - 1], own))
-        for known, new in zip((here, beside, across), from_neighbours(masked[w], upper[w])):
-            known.append(new)
+            upper[w], own, slots, keep = lax.optimization_barrier((upper[w], own, slots, keep))
+        beside.append(to_core(masked[w], upper[w]))
+        if w:
+            upper[w], beside[w - 1] = lax.optimization_barrier((upper[w], beside[w - 1]))
+        across.append(to_pair(masked[w], upper[w]))
+        here.append(jnp.where(place == 0, masked[w], upper[w]))
     across[0], beside[-1] = lax.optimization_barrier((across[0], beside[-1]))
     shape = (width, windows * depth, lanes)
     first = call(
@@ -443,9 +468,6 @@
     across[-1], first = lax.optimization_barrier((across[-1], first))
     across_beside = [send(block, lambda q, p, c, g: (q, p, 1 - c, g)) for block in across]
     early = [first]
-    slots = jnp.stack([0, 1 + 2 * core, 2, 3 - 2 * core]).astype(jnp.int32)
-    offset_ids = place * owned + slots
-    keep = jnp.where(offset_ids < reach[0], jnp.float32(scale), jnp.float32(0.0))
     result = call(
         functools.partial(last_kernel, windows, len(early)), "second_pair",
         [r for both in zip(across, across_beside) for r in both],

time: 72.6 us -> 74.4 us (1.025)
  waiting for transfers between devices: 17.8 us -> 14.8 us
  Pallas kernels: 35.2 us -> 37.7 us
  local copies, waits for them, and re-layouts: 0.01 us -> 2.08 us
    ppermute x8, waiting for transfers between devices: 17.8 us -> 14.8 us  [send(): return lax.ppermute(payload, ('fibre', 'freq'), pairs)]
    pallas_call x0 -> x1, Pallas kernels: none -> 2.48 us  [per_device(): pl.pallas_call(mask_kernel, out_shape=[jax.ShapeDtypeStruct((channels, sa...]
    unnamed x2 -> x8, local copies, waits for them, and re-layouts: 0.01 us -> 2.08 us
    select_n x3 -> x2, other arithmetic: 1.55 us -> 2.23 us  [per_device(): here.append(jnp.where(place == 0, masked[w], upper[w]))]
  transfers between devices with their start and end apart: 8 -> 8, of which waited for: 4 -> 4; matrix products, arithmetic and copies ran while one was open for 0% -> 3% of each run, Pallas kernels for 26% -> 25%
where the time goes in v1:
time: 74.4 us; the launch traced here: 74 us
  Pallas kernels  37.7 us (51%)
  starting transfers between devices  16.3 us (22%)
  waiting for transfers between devices  14.8 us (20%)
  other arithmetic  2.31 us (3%)
  local copies, waits for them, and re-layouts  2.08 us (3%)
  between operations  0.83 us (1%)
    pallas_call x4, Pallas kernels, call(): pl.pallas_call(kernel, out_shape=out_shape, in_specs=[vmem_spec] * len(op...  35.2 us
    ppermute x8, starting transfers between devices, send(): return lax.ppermute(payload, ('fibre', 'freq'), pairs)  16.3 us
    ppermute x8, waiting for transfers between devices, send(): return lax.ppermute(payload, ('fibre', 'freq'), pairs)  14.8 us
    pallas_call x1, Pallas kernels, per_device(): pl.pallas_call(mask_kernel, out_shape=[jax.ShapeDtypeStruct((channels, sa...  2.48 us
    select_n x2, other arithmetic, per_device(): here.append(jnp.where(place == 0, masked[w], upper[w]))  2.23 us
    unnamed x8, local copies, waits for them, and re-layouts  2.08 us
  transfers between devices with their start and end apart: 8, of which 4 were waited for; matrix products, arithmetic and copies ran while one was open for 3% of the time, Pallas kernels for 25%

profile of v1, /device:TPU:21, one launch (start us, length us, event | category | flops | bytes accessed | tf_op | source)
XLA Modules:
  0.0 74.0 jit_solution(2074975354495337493)
XLA Ops:
  0.0 2.5 %mask_dead.1 = (bf16[64,4096]{1,0:T(8,128)(2,1)}, bf16[64,4096]{1,0:T(8,128)(2,1)}) custom-call(bf16[2,64,4096]{2,1,0:T(8,128)(2,1)} %traces_ref.1, s32[1,64]{1,0:T(1,128)} %bitcast.6), custom_call_target="tpu_custom_call" | custom-call | tf_op jit(solution)/shard_map/mask_dead/pallas_call | solution.py:383
  2.5 2.1 %collective-permute-start = (bf16[64,4096]{1,0:T(8,128)(2,1)}, bf16[64,4096]{1,0:T(8,128)(2,1)S(1)}, u32[]{:S(2)}, u32[]{:S(2)}) collective-permute-start(bf16[64,4096]{1,0:T(8,128)(2,1)} %get-tuple-element.19.refs_0_), channel_id=1, source_target_pairs={{8,0},{9,1},{10,2},{11,3},{12,4},{13,5},{15,7},{16,8},{17,9},{18,1... | collective-permute-start | bytes 1572872 | tf_op jit(solution)/shard_map/ppermute | solution.py:409
  4.6 2.1 %collective-permute-start.2 = (bf16[64,4096]{1,0:T(8,128)(2,1)}, bf16[64,4096]{1,0:T(8,128)(2,1)}, u32[]{:S(2)}, u32[]{:S(2)}) collective-permute-start(bf16[64,4096]{1,0:T(8,128)(2,1)} %get-tuple-element.20.refs_1_), channel_id=1, source_target_pairs={{8,0},{9,1},{10,2},{11,3},{12,4},{13,5},{15,7},{16,8},{17,9},{18,1... | collective-permute-start | bytes 1572872 | tf_op jit(solution)/shard_map/ppermute | solution.py:409
  6.7 0.0 copy-start
  6.7 1.0 %copy-done = bf16[64,4096]{1,0:T(8,128)(2,1)S(1)} copy-done((bf16[64,4096]{1,0:T(8,128)(2,1)S(1)}, bf16[64,4096]{1,0:T(8,128)(2,1)}, u32[]{:S(2)}) %copy-start) | copy-done | bytes 524312
  7.7 0.0 copy-start.2
  7.7 1.0 %copy-done.2 = bf16[64,4096]{1,0:T(8,128)(2,1)S(1)} copy-done((bf16[64,4096]{1,0:T(8,128)(2,1)S(1)}, bf16[64,4096]{1,0:T(8,128)(2,1)}, u32[]{:S(2)}) %copy-start.2) | copy-done | bytes 524312
  8.8 4.5 %own_spectra.1.white_ref = bf16[16,256,256]{2,1,0:T(8,128)(2,1)S(1)} custom-call(bf16[64,4096]{1,0:T(8,128)(2,1)S(1)} %copy-done.2, bf16[64,4096]{1,0:T(8,128)(2,1)S(1)} %copy-done, bf16[16,256,256]{2,1,0:T(8,128)(2,1)} %constant.63.clone.refs_2_.refs_4_, bf16[16,256,256]{2,1,0:T(8,128)(2,1)} %constant.64.clone.refs_3_.refs_5_), custom_call_target="tpu_custom_call" | custom-call | flops 2147483648 | bytes 14680064 | tf_op jit(solution)/shard_map/own_spectra/pallas_call | solution.py:361
  13.3 4.1 %collective-permute-done = bf16[64,4096]{1,0:T(8,128)(2,1)S(1)} collective-permute-done((bf16[64,4096]{1,0:T(8,128)(2,1)}, bf16[64,4096]{1,0:T(8,128)(2,1)S(1)}, u32[]{:S(2)}, u32[]{:S(2)}) %collective-permute-start) | collective-permute-done | bytes 524320 | tf_op jit(solution)/shard_map/ppermute | solution.py:409
  17.4 1.1 %broadcast_select_fusion.1 = (bf16[64,4096]{1,0:T(8,128)(2,1)S(1)}, bf16[64,4096]{1,0:T(8,128)(2,1)}, bf16[64,4096]{1,0:T(8,128)(2,1)}) fusion(bf16[64,4096]{1,0:T(8,128)(2,1)S(1)} %copy-done.2, bf16[64,4096]{1,0:T(8,128)(2,1)S(1)} %collective-permute-done, pred[]{:T(512)S(6)} %eq.10, pred[]{:T(512)S(6)} %and.28, pred[]{:T(512)S(6)} %and.26), kind=kLoop, calls=%fused_computation.1 | loop fusion | flops 786432 | bytes 2621443 | tf_op jit(solution)/shard_map/jit(_where)/select_n | solution.py:459
  18.4 4.6 %collective-permute-start.5 = (bf16[64,4096]{1,0:T(8,128)(2,1)}, bf16[64,4096]{1,0:T(8,128)(2,1)S(1)}, u32[]{:S(2)}, u32[]{:S(2)}) collective-permute-start(bf16[64,4096]{1,0:T(8,128)(2,1)} %get-tuple-element.38), channel_id=1, source_target_pairs={{2,0},{3,1},{1,2},{8,3},{6,4},{7,5},{5,6},{12,7},{10,8},{11,9},{9,... | collective-permute-start | bytes 1572872 | tf_op jit(solution)/shard_map/ppermute | solution.py:409
  23.7 0.1 compare_select_fusion
  23.8 0.0 copy-start.1
  23.8 3.1 %collective-permute-start.1 = (bf16[64,4096]{1,0:T(8,128)(2,1)}, bf16[64,4096]{1,0:T(8,128)(2,1)S(1)}, u32[]{:S(2)}, u32[]{:S(2)}) collective-permute-start(bf16[64,4096]{1,0:T(8,128)(2,1)} %get-tuple-element.39), channel_id=1, source_target_pairs={{4,0},{5,1},{6,2},{7,3},{0,4},{9,5},{2,6},{11,7},{12,8},{13,9},{14... | collective-permute-start | bytes 1572872 | tf_op jit(solution)/shard_map/ppermute | solution.py:409
  26.9 6.4 %own_bins.1.refs_7_ = bf16[128,128,128]{2,1,0:T(8,128)(2,1)} custom-call(bf16[16,256,256]{2,1,0:T(8,128)(2,1)S(1)} %own_spectra.1.white_ref, bf16[16,512,256]{2,1,0:T(8,128)(2,1)} %constant.65.clone.bins_hbm), custom_call_target="tpu_custom_call" | custom-call | flops 2147483648 | bytes 14680064 | tf_op jit(solution)/shard_map/own_bins/pallas_call | solution.py:361
  33.3 0.0 collective-permute-done.2
  33.3 1.7 %collective-permute-done.5.refs_1_ = bf16[64,4096]{1,0:T(8,128)(2,1)S(1)} collective-permute-done((bf16[64,4096]{1,0:T(8,128)(2,1)}, bf16[64,4096]{1,0:T(8,128)(2,1)S(1)}, u32[]{:S(2)}, u32[]{:S(2)}) %collective-permute-start.5) | collective-permute-done | bytes 524320 | tf_op jit(solution)/shard_map/ppermute | solution.py:409
  35.0 0.0 copy-done.1
  35.0 1.2 %broadcast_select_fusion = (bf16[64,4096]{1,0:T(8,128)(2,1)S(1)}, bf16[64,4096]{1,0:T(8,128)(2,1)S(1)}, bf16[64,4096]{1,0:T(8,128)(2,1)S(1)}) fusion(bf16[64,4096]{1,0:T(8,128)(2,1)S(1)} %copy-done.1, bf16[64,4096]{1,0:T(8,128)(2,1)} %collective-permute-done.2, pred[]{:T(512)S(6)} %eq.10, pred[]{:T(512)S(6)} %and.26, pred[]{:T(512)S(6)} %and.28), kind=kLoop, calls=%fused_computation | loop fusion | flops 786432 | bytes 2621443 | tf_op jit(solution)/shard_map/jit(_where)/select_n | solution.py:459
  36.2 1.9 %collective-permute-start.3 = (bf16[64,4096]{1,0:T(8,128)(2,1)S(1)}, bf16[64,4096]{1,0:T(8,128)(2,1)S(1)}, u32[]{:S(2)}, u32[]{:S(2)}) collective-permute-start(bf16[64,4096]{1,0:T(8,128)(2,1)S(1)} %get-tuple-element.40), channel_id=1, source_target_pairs={{2,0},{3,1},{1,2},{8,3},{6,4},{7,5},{5,6},{12,7},{10,8},{11,9},{9,... | collective-permute-start | bytes 1572872 | tf_op jit(solution)/shard_map/ppermute | solution.py:409
  38.1 1.9 %collective-permute-start.6 = (bf16[64,4096]{1,0:T(8,128)(2,1)S(1)}, bf16[64,4096]{1,0:T(8,128)(2,1)S(1)}, u32[]{:S(2)}, u32[]{:S(2)}) collective-permute-start(bf16[64,4096]{1,0:T(8,128)(2,1)S(1)} %get-tuple-element.36), channel_id=1, source_target_pairs={{4,0},{5,1},{6,2},{7,3},{0,4},{9,5},{2,6},{11,7},{12,8},{13,9},{14... | collective-permute-start | bytes 1572872 | tf_op jit(solution)/shard_map/ppermute | solution.py:409
  40.0 0.0 collective-permute-done.1.refs_0_
  40.0 7.5 %collective-permute-done.3.refs_3_ = bf16[64,4096]{1,0:T(8,128)(2,1)S(1)} collective-permute-done((bf16[64,4096]{1,0:T(8,128)(2,1)S(1)}, bf16[64,4096]{1,0:T(8,128)(2,1)S(1)}, u32[]{:S(2)}, u32[]{:S(2)}) %collective-permute-start.3) | collective-permute-done | bytes 524320 | tf_op jit(solution)/shard_map/ppermute | solution.py:409
  47.6 0.0 collective-permute-start.4
  47.6 0.0 copy-start.3
  47.6 7.9 %first_pair.1.refs_8_ = bf16[128,128,128]{2,1,0:T(8,128)(2,1)} custom-call(bf16[64,4096]{1,0:T(8,128)(2,1)S(1)} %get-tuple-element.37.refs_0_, bf16[64,4096]{1,0:T(8,128)(2,1)S(1)} %collective-permute-done.5.refs_1_, bf16[64,4096]{1,0:T(8,128)(2,1)S(1)} %get-tuple-element.35.refs_2_, bf16[64,4096]{1,0:T(8,128)(2,1)S(1)} %collective-permute-done.3.refs_3_, ...), custom_call_target="tpu_custom_call" | custom-call | flops 4294967296 | bytes 14680064 | tf_op jit(solution)/shard_map/first_pair/pallas_call | solution.py:361
  55.5 0.0 collective-permute-done.6.refs_2_
  55.5 0.6 collective-permute-start.7
  56.0 0.0 collective-permute-done.4.refs_1_
  56.0 1.5 %collective-permute-done.7.refs_3_ = bf16[64,4096]{1,0:T(8,128)(2,1)S(1)} collective-permute-done((bf16[64,4096]{1,0:T(8,128)(2,1)S(1)}, bf16[64,4096]{1,0:T(8,128)(2,1)S(1)}, u32[]{:S(2)}, u32[]{:S(2)}) %collective-permute-start.7) | collective-permute-done | bytes 524320 | tf_op jit(solution)/shard_map/ppermute | solution.py:409
  57.6 0.0 copy-done.3
  57.6 16.4 %second_pair.1 = f32[4,64,64,128]{3,2,1,0:T(8,128)} custom-call(bf16[64,4096]{1,0:T(8,128)(2,1)S(1)} %collective-permute-done.1.refs_0_, bf16[64,4096]{1,0:T(8,128)(2,1)S(1)} %collective-permute-done.4.refs_1_, bf16[64,4096]{1,0:T(8,128)(2,1)S(1)} %collective-permute-done.6.refs_2_, bf16[64,4096]{1,0:T(8,128)(2,1)S(1)} %collective-permute-done.7.refs_3_, ...), custom_call_target="tpu_custom_call" | custom-call | flops 8589934592 | bytes 14680064 | tf_op jit(solution)/shard_map/second_pair/pallas_call | solution.py:361
Async XLA Ops:
  2.5 14.9 %collective-permute-start = (bf16[64,4096]{1,0:T(8,128)(2,1)}, bf16[64,4096]{1,0:T(8,128)(2,1)S(1)}, u32[]{:S(2)}, u32[]{:S(2)}) collective-permute-start(bf16[64,4096]{1,0:T(8,128)(2,1)} %get-tuple-element.19.refs_0_), channel_id=1, source_target_pairs={{8,0},{9,1},{10,2},{11,3},{12,4},{13,5},{15,7},{16,8},{17,9},{18,1... | collective-permute-start | bytes 1572872 | tf_op jit(solution)/shard_map/ppermute | solution.py:409
  4.6 28.7 %collective-permute-start.2 = (bf16[64,4096]{1,0:T(8,128)(2,1)}, bf16[64,4096]{1,0:T(8,128)(2,1)}, u32[]{:S(2)}, u32[]{:S(2)}) collective-permute-start(bf16[64,4096]{1,0:T(8,128)(2,1)} %get-tuple-element.20.refs_1_), channel_id=1, source_target_pairs={{8,0},{9,1},{10,2},{11,3},{12,4},{13,5},{15,7},{16,8},{17,9},{18,1... | collective-permute-start | bytes 1572872 | tf_op jit(solution)/shard_map/ppermute | solution.py:409
  6.7 1.0 %copy-start = (bf16[64,4096]{1,0:T(8,128)(2,1)S(1)}, bf16[64,4096]{1,0:T(8,128)(2,1)}, u32[]{:S(2)}) copy-start(bf16[64,4096]{1,0:T(8,128)(2,1)} %get-tuple-element.20.refs_1_) | copy-start | bytes 1572868
  7.7 1.0 %copy-start.2 = (bf16[64,4096]{1,0:T(8,128)(2,1)S(1)}, bf16[64,4096]{1,0:T(8,128)(2,1)}, u32[]{:S(2)}) copy-start(bf16[64,4096]{1,0:T(8,128)(2,1)} %get-tuple-element.19.refs_0_) | copy-start | bytes 1572868
  18.4 16.6 %collective-permute-start.5 = (bf16[64,4096]{1,0:T(8,128)(2,1)}, bf16[64,4096]{1,0:T(8,128)(2,1)S(1)}, u32[]{:S(2)}, u32[]{:S(2)}) collective-permute-start(bf16[64,4096]{1,0:T(8,128)(2,1)} %get-tuple-element.38), channel_id=1, source_target_pairs={{2,0},{3,1},{1,2},{8,3},{6,4},{7,5},{5,6},{12,7},{10,8},{11,9},{9,... | collective-permute-start | bytes 1572872 | tf_op jit(solution)/shard_map/ppermute | solution.py:409
  23.8 11.2 %copy-start.1 = (bf16[64,4096]{1,0:T(8,128)(2,1)S(1)}, bf16[64,4096]{1,0:T(8,128)(2,1)}, u32[]{:S(2)}) copy-start(bf16[64,4096]{1,0:T(8,128)(2,1)} %get-tuple-element.20.refs_1_) | copy-start | bytes 1572868
  23.8 16.2 %collective-permute-start.1 = (bf16[64,4096]{1,0:T(8,128)(2,1)}, bf16[64,4096]{1,0:T(8,128)(2,1)S(1)}, u32[]{:S(2)}, u32[]{:S(2)}) collective-permute-start(bf16[64,4096]{1,0:T(8,128)(2,1)} %get-tuple-element.39), channel_id=1, source_target_pairs={{4,0},{5,1},{6,2},{7,3},{0,4},{9,5},{2,6},{11,7},{12,8},{13,9},{14... | collective-permute-start | bytes 1572872 | tf_op jit(solution)/shard_map/ppermute | solution.py:409
  36.2 11.4 %collective-permute-start.3 = (bf16[64,4096]{1,0:T(8,128)(2,1)S(1)}, bf16[64,4096]{1,0:T(8,128)(2,1)S(1)}, u32[]{:S(2)}, u32[]{:S(2)}) collective-permute-start(bf16[64,4096]{1,0:T(8,128)(2,1)S(1)} %get-tuple-element.40), channel_id=1, source_target_pairs={{2,0},{3,1},{1,2},{8,3},{6,4},{7,5},{5,6},{12,7},{10,8},{11,9},{9,... | collective-permute-start | bytes 1572872 | tf_op jit(solution)/shard_map/ppermute | solution.py:409
  38.1 17.4 %collective-permute-start.6 = (bf16[64,4096]{1,0:T(8,128)(2,1)S(1)}, bf16[64,4096]{1,0:T(8,128)(2,1)S(1)}, u32[]{:S(2)}, u32[]{:S(2)}) collective-permute-start(bf16[64,4096]{1,0:T(8,128)(2,1)S(1)} %get-tuple-element.36), channel_id=1, source_target_pairs={{4,0},{5,1},{6,2},{7,3},{0,4},{9,5},{2,6},{11,7},{12,8},{13,9},{14... | collective-permute-start | bytes 1572872 | tf_op jit(solution)/shard_map/ppermute | solution.py:409
  47.6 8.5 %collective-permute-start.4 = (bf16[64,4096]{1,0:T(8,128)(2,1)S(1)}, bf16[64,4096]{1,0:T(8,128)(2,1)S(1)}, u32[]{:S(2)}, u32[]{:S(2)}) collective-permute-start(bf16[64,4096]{1,0:T(8,128)(2,1)S(1)} %collective-permute-done.1.refs_0_), channel_id=1, source_target_pairs={{2,0},{3,1},{0,2},{1,3},{6,4},{7,5},{4,6},{5,7},{10,8},{11,9},{8,1... | collective-permute-start | bytes 1572872 | tf_op jit(solution)/shard_map/ppermute | solution.py:409
  47.6 10.0 %copy-start.3 = (bf16[128,256]{1,0:T(8,128)(2,1)S(1)}, bf16[128,256]{1,0:T(8,128)(2,1)}, u32[]{:S(2)}) copy-start(bf16[128,256]{1,0:T(8,128)(2,1)} %constant.67.clone.refs_9_) | copy-start | bytes 196612
  55.5 2.1 %collective-permute-start.7 = (bf16[64,4096]{1,0:T(8,128)(2,1)S(1)}, bf16[64,4096]{1,0:T(8,128)(2,1)S(1)}, u32[]{:S(2)}, u32[]{:S(2)}) collective-permute-start(bf16[64,4096]{1,0:T(8,128)(2,1)S(1)} %collective-permute-done.6.refs_2_), channel_id=1, source_target_pairs={{2,0},{3,1},{0,2},{1,3},{6,4},{7,5},{4,6},{5,7},{10,8},{11,9},{8,1... | collective-permute-start | bytes 1572872 | tf_op jit(solution)/shard_map/ppermute | solution.py:409

commit v2 on v0

--- a/solution.py
+++ b/solution.py
@@ -125,7 +125,7 @@
     return out
 
 
-def whiten(copies_of, records, copies, fhi, flo, yhi, ylo, spec):
+def whiten(copies_of, records, copies, fhi, flo, yhi, ylo, spec, later=()):
     channels, samples = records[0].shape
     width = LAGS
     residues = samples // width
@@ -155,6 +155,8 @@
     lax.fori_loop(0, channels // step, transform, 0)
     copies[0].wait()
     copies[1].wait()
+    for copy in later:
+        copy.start()
     nt = (((1,), (1,)), ((), ()))
     bands = (samples // 2) // BAND
 
@@ -181,11 +183,15 @@
     return white
 
 
-def start_copies(sources, targets, sems):
-    copies = [
+def make_copies(sources, targets, sems):
+    return [
         pltpu.make_async_copy(source, target, sems.at[i])
         for i, (source, target) in enumerate(zip(sources, targets))
     ]
+
+
+def start_copies(sources, targets, sems):
+    copies = make_copies(sources, targets, sems)
     for copy in copies:
         copy.start()
     return copies
@@ -273,8 +279,10 @@
 def pair_kernel(windows, *refs):
     records, sources, refs = refs[:2 * windows], refs[2 * windows:2 * windows + 3], refs[2 * windows + 3:]
     out_hbm, fhi, flo, bins, yhi, ylo, spec, *wide, stage, sems, out_sems = refs
-    copies = start_copies(sources, (fhi, flo, bins), sems)
-    white = whiten(1, records, copies, fhi, flo, yhi, ylo, spec)
+    copies = make_copies(sources, (fhi, flo, bins), sems)
+    copies[0].start()
+    copies[1].start()
+    white = whiten(1, records, copies, fhi, flo, yhi, ylo, spec, copies[2:])
     copies[2].wait()
     fill_bins(white, bins, wide)
     depth = stage.shape[1] // windows
@@ -288,12 +296,24 @@
     loaded, (yhi, ylo, *scratch) = scratch[:count], scratch[count:]
     wide, cross, (stage, sems, out_sems) = scratch[:windows], scratch[windows:windows + pairs], scratch[windows + pairs:]
     fhi, flo, bins, own_ref, *early = loaded
-    copies = start_copies(sources, loaded, sems)
-    white = whiten(1, records, copies, fhi, flo, yhi, ylo, cross[0])
-    copies[2].wait()
+    tables = make_copies(sources[:3], loaded[:3], sems)
+    tables[0].start()
+    tables[1].start()
+    splits = (sems.shape[0] - 3) // (1 + earlier)
+    per_split = own_ref.shape[0] // splits
+    chunks = []
+    for split in range(splits):
+        part = pl.ds(split * per_split, per_split)
+        chunks.append([
+            pltpu.make_async_copy(source.at[part], target.at[part], sems.at[3 + split * (1 + earlier) + i])
+            for i, (source, target) in enumerate(zip(sources[3:], loaded[3:]))
+        ])
+    white = whiten(1, records, tables, fhi, flo, yhi, ylo, cross[0], [tables[2]] + chunks[0])
+    tables[2].wait()
+    for chunk in chunks[1:]:
+        for copy in chunk:
+            copy.start()
     fill_bins(white, bins, wide)
-    for copy in copies[3:]:
-        copy.wait()
     width, lanes, _ = own_ref.shape
     channels = lanes // 2
     depth = bins.shape[0] * 4
@@ -308,10 +328,13 @@
                 )
         return carry
 
-    lax.fori_loop(0, width, one_bin, 0, unroll=16)
+    for split, chunk in enumerate(chunks):
+        for copy in chunk:
+            copy.wait()
+        lax.fori_loop(split * per_split, (split + 1) * per_split, one_bin, 0, unroll=16)
     rows = 2 * width
     _, offsets, per_out, channels, _ = stage.shape
-    chunks = channels // per_out
+    out_chunks = channels // per_out
 
     def leave(chunk, slot):
         target = out_hbm.at[:, pl.ds(chunk * per_out, per_out)]
@@ -339,9 +362,9 @@
             leave(chunk, slot).start()
         return carry
 
-    lax.fori_loop(0, chunks // 2, two_chunks, 0)
+    lax.fori_loop(0, out_chunks // 2, two_chunks, 0)
     for slot in range(2):
-        leave(chunks - 2 + slot, slot).wait()
+        leave(out_chunks - 2 + slot, slot).wait()
 
 
 def call(kernel, name, operands, streamed, small, out_shape, out_space, scratch, flops, limit=50):
@@ -453,7 +476,7 @@
         jax.ShapeDtypeStruct((owned, channels, channels, LAGS), f32), pl.ANY,
         table_shapes + [pltpu.VMEM(own_shape, bf16)] + [pltpu.VMEM(e.shape, bf16) for e in early]
         + split_shapes + wide_shapes + [pltpu.VMEM((channels * (2 * width + 1), lanes), f32)] * pairs
-        + [pltpu.VMEM((2, owned, channels // 8, channels, LAGS), f32), dma((4 + len(early),)), dma((2,))],
+        + [pltpu.VMEM((2, owned, channels // 8, channels, LAGS), f32), dma((3 + 4 * (1 + len(early)),)), dma((2,))],
         2 * work,
     )
     return result[None]

time: 72.6 us -> 72.8 us (level)
  no operation moved by 1% of the time
where the time goes in v2:
time: 72.8 us; the launch traced here: 72.5 us
  Pallas kernels  35.4 us (49%)
  waiting for transfers between devices  17.8 us (24%)
  starting transfers between devices  16.2 us (22%)
  other arithmetic  2.29 us (3%)
  between operations  0.82 us (1%)
    pallas_call x4, Pallas kernels, call(): pl.pallas_call(kernel, out_shape=out_shape, in_specs=[vmem_spec] * len(op...  35.4 us
    ppermute x8, waiting for transfers between devices, send(): return lax.ppermute(payload, ('fibre', 'freq'), pairs)  17.8 us
    ppermute x8, starting transfers between devices, send(): return lax.ppermute(payload, ('fibre', 'freq'), pairs)  16.2 us
  transfers between devices with their start and end apart: 8, of which 4 were waited for; matrix products, arithmetic and copies ran while one was open for 0% of the time, Pallas kernels for 26%

profile of v2, /device:TPU:21, one launch (start us, length us, event | category | flops | bytes accessed | tf_op | source)
XLA Modules:
  0.0 72.5 jit_solution(3784000177341328648)
XLA Ops:
  0.0 0.7 broadcast_compare_fusion
  0.7 1.3 %bitcast_select_fusion = (bf16[64,4096]{1,0:T(8,128)(2,1)S(1)}, bf16[64,4096]{1,0:T(8,128)(2,1)S(1)}) fusion(bf16[2,64,4096]{2,1,0:T(8,128)(2,1)} %param.8, pred[64]{0:T(512)(128)(4,1)S(1)} %broadcast_compare_fusion), kind=kLoop, calls=%fused_computation | loop fusion | flops 524288 | bytes 2097216 | tf_op jit(solution)/shard_map/jit(_where)/select_n | solution.py:395
  2.0 2.1 %collective-permute-start = (bf16[64,4096]{1,0:T(8,128)(2,1)S(1)}, bf16[64,4096]{1,0:T(8,128)(2,1)S(1)}, u32[]{:S(2)}, u32[]{:S(2)}) collective-permute-start(bf16[64,4096]{1,0:T(8,128)(2,1)S(1)} %get-tuple-element.26.refs_0_), channel_id=1, source_target_pairs={{8,0},{9,1},{10,2},{11,3},{12,4},{13,5},{15,7},{16,8},{17,9},{18,1... | collective-permute-start | bytes 1572872 | tf_op jit(solution)/shard_map/ppermute | solution.py:414
  4.1 2.1 %collective-permute-start.2 = (bf16[64,4096]{1,0:T(8,128)(2,1)S(1)}, bf16[64,4096]{1,0:T(8,128)(2,1)S(1)}, u32[]{:S(2)}, u32[]{:S(2)}) collective-permute-start(bf16[64,4096]{1,0:T(8,128)(2,1)S(1)} %get-tuple-element.25.refs_1_), channel_id=1, source_target_pairs={{8,0},{9,1},{10,2},{11,3},{12,4},{13,5},{15,7},{16,8},{17,9},{18,1... | collective-permute-start | bytes 1572872 | tf_op jit(solution)/shard_map/ppermute | solution.py:414
  6.2 4.5 %own_spectra.1.white_ref = bf16[16,256,256]{2,1,0:T(8,128)(2,1)S(1)} custom-call(bf16[64,4096]{1,0:T(8,128)(2,1)S(1)} %get-tuple-element.26.refs_0_, bf16[64,4096]{1,0:T(8,128)(2,1)S(1)} %get-tuple-element.25.refs_1_, bf16[16,256,256]{2,1,0:T(8,128)(2,1)} %constant.66.clone.refs_2_.refs_4_, bf16[16,256,256]{2,1,0:T(8,128)(2,1)} %constant.67.clone.refs_3_.refs_5_), custom_call_target="tpu_custom_call" | custom-call | flops 2147483648 | bytes 14680064 | tf_op jit(solution)/shard_map/own_spectra/pallas_call | solution.py:373
  10.8 5.9 %collective-permute-done = bf16[64,4096]{1,0:T(8,128)(2,1)S(1)} collective-permute-done((bf16[64,4096]{1,0:T(8,128)(2,1)S(1)}, bf16[64,4096]{1,0:T(8,128)(2,1)S(1)}, u32[]{:S(2)}, u32[]{:S(2)}) %collective-permute-start) | collective-permute-done | bytes 524320 | tf_op jit(solution)/shard_map/ppermute | solution.py:414
  16.7 0.1 broadcast_select_fusion.1
  16.8 4.6 %collective-permute-start.3 = (bf16[64,4096]{1,0:T(8,128)(2,1)S(1)}, bf16[64,4096]{1,0:T(8,128)(2,1)S(1)}, u32[]{:S(2)}, u32[]{:S(2)}) collective-permute-start(bf16[64,4096]{1,0:T(8,128)(2,1)S(1)} %get-tuple-element.31), channel_id=1, source_target_pairs={{2,0},{3,1},{1,2},{8,3},{6,4},{7,5},{5,6},{12,7},{10,8},{11,9},{9,... | collective-permute-start | bytes 1572872 | tf_op jit(solution)/shard_map/ppermute | solution.py:414
  21.4 3.0 %collective-permute-start.1 = (bf16[64,4096]{1,0:T(8,128)(2,1)S(1)}, bf16[64,4096]{1,0:T(8,128)(2,1)S(1)}, u32[]{:S(2)}, u32[]{:S(2)}) collective-permute-start(bf16[64,4096]{1,0:T(8,128)(2,1)S(1)} %get-tuple-element.32), channel_id=1, source_target_pairs={{4,0},{5,1},{6,2},{7,3},{0,4},{9,5},{2,6},{11,7},{12,8},{13,9},{14... | collective-permute-start | bytes 1572872 | tf_op jit(solution)/shard_map/ppermute | solution.py:414
  24.4 6.4 %own_bins.1.refs_7_ = bf16[128,128,128]{2,1,0:T(8,128)(2,1)} custom-call(bf16[16,256,256]{2,1,0:T(8,128)(2,1)S(1)} %own_spectra.1.white_ref, bf16[16,512,256]{2,1,0:T(8,128)(2,1)} %constant.68.clone.bins_hbm), custom_call_target="tpu_custom_call" | custom-call | flops 2147483648 | bytes 14680064 | tf_op jit(solution)/shard_map/own_bins/pallas_call | solution.py:373
  30.8 0.0 collective-permute-done.2
  30.8 3.5 %collective-permute-done.3.refs_1_ = bf16[64,4096]{1,0:T(8,128)(2,1)S(1)} collective-permute-done((bf16[64,4096]{1,0:T(8,128)(2,1)S(1)}, bf16[64,4096]{1,0:T(8,128)(2,1)S(1)}, u32[]{:S(2)}, u32[]{:S(2)}) %collective-permute-start.3) | collective-permute-done | bytes 524320 | tf_op jit(solution)/shard_map/ppermute | solution.py:414
  34.3 0.1 broadcast_select_fusion
  34.5 1.9 %collective-permute-start.4 = (bf16[64,4096]{1,0:T(8,128)(2,1)S(1)}, bf16[64,4096]{1,0:T(8,128)(2,1)S(1)}, u32[]{:S(2)}, u32[]{:S(2)}) collective-permute-start(bf16[64,4096]{1,0:T(8,128)(2,1)S(1)} %get-tuple-element.29), channel_id=1, source_target_pairs={{2,0},{3,1},{1,2},{8,3},{6,4},{7,5},{5,6},{12,7},{10,8},{11,9},{9,... | collective-permute-start | bytes 1572872 | tf_op jit(solution)/shard_map/ppermute | solution.py:414
  36.4 1.9 %collective-permute-start.6 = (bf16[64,4096]{1,0:T(8,128)(2,1)S(1)}, bf16[64,4096]{1,0:T(8,128)(2,1)S(1)}, u32[]{:S(2)}, u32[]{:S(2)}) collective-permute-start(bf16[64,4096]{1,0:T(8,128)(2,1)S(1)} %get-tuple-element.28), channel_id=1, source_target_pairs={{4,0},{5,1},{6,2},{7,3},{0,4},{9,5},{2,6},{11,7},{12,8},{13,9},{14... | collective-permute-start | bytes 1572872 | tf_op jit(solution)/shard_map/ppermute | solution.py:414
  38.3 0.0 collective-permute-done.1.refs_0_
  38.3 7.5 %collective-permute-done.4.refs_3_ = bf16[64,4096]{1,0:T(8,128)(2,1)S(1)} collective-permute-done((bf16[64,4096]{1,0:T(8,128)(2,1)S(1)}, bf16[64,4096]{1,0:T(8,128)(2,1)S(1)}, u32[]{:S(2)}, u32[]{:S(2)}) %collective-permute-start.4) | collective-permute-done | bytes 524320 | tf_op jit(solution)/shard_map/ppermute | solution.py:414
  45.9 0.0 collective-permute-start.5
  45.9 0.0 copy-start
  45.9 8.0 %first_pair.1.refs_8_ = bf16[128,128,128]{2,1,0:T(8,128)(2,1)} custom-call(bf16[64,4096]{1,0:T(8,128)(2,1)S(1)} %get-tuple-element.30.refs_0_, bf16[64,4096]{1,0:T(8,128)(2,1)S(1)} %collective-permute-done.3.refs_1_, bf16[64,4096]{1,0:T(8,128)(2,1)S(1)} %get-tuple-element.27.refs_2_, bf16[64,4096]{1,0:T(8,128)(2,1)S(1)} %collective-permute-done.4.refs_3_, ...), custom_call_target="tpu_custom_call" | custom-call | flops 4294967296 | bytes 14680064 | tf_op jit(solution)/shard_map/first_pair/pallas_call | solution.py:373
  53.9 0.0 collective-permute-done.6.refs_2_
  53.9 0.6 collective-permute-start.7
  55.1 0.1 compare_select_fusion
  55.2 0.0 collective-permute-done.5.refs_1_
  55.2 0.8 %collective-permute-done.7.refs_3_ = bf16[64,4096]{1,0:T(8,128)(2,1)S(1)} collective-permute-done((bf16[64,4096]{1,0:T(8,128)(2,1)S(1)}, bf16[64,4096]{1,0:T(8,128)(2,1)S(1)}, u32[]{:S(2)}, u32[]{:S(2)}) %collective-permute-start.7) | collective-permute-done | bytes 524320 | tf_op jit(solution)/shard_map/ppermute | solution.py:414
  56.0 0.0 copy-done
  56.0 16.5 %second_pair.1 = f32[4,64,64,128]{3,2,1,0:T(8,128)} custom-call(bf16[64,4096]{1,0:T(8,128)(2,1)S(1)} %collective-permute-done.1.refs_0_, bf16[64,4096]{1,0:T(8,128)(2,1)S(1)} %collective-permute-done.5.refs_1_, bf16[64,4096]{1,0:T(8,128)(2,1)S(1)} %collective-permute-done.6.refs_2_, bf16[64,4096]{1,0:T(8,128)(2,1)S(1)} %collective-permute-done.7.refs_3_, ...), custom_call_target="tpu_custom_call" | custom-call | flops 8589934592 | bytes 14680064 | tf_op jit(solution)/shard_map/second_pair/pallas_call | solution.py:373
Async XLA Ops:
  2.0 14.7 %collective-permute-start = (bf16[64,4096]{1,0:T(8,128)(2,1)S(1)}, bf16[64,4096]{1,0:T(8,128)(2,1)S(1)}, u32[]{:S(2)}, u32[]{:S(2)}) collective-permute-start(bf16[64,4096]{1,0:T(8,128)(2,1)S(1)} %get-tuple-element.26.refs_0_), channel_id=1, source_target_pairs={{8,0},{9,1},{10,2},{11,3},{12,4},{13,5},{15,7},{16,8},{17,9},{18,1... | collective-permute-start | bytes 1572872 | tf_op jit(solution)/shard_map/ppermute | solution.py:414
  4.1 26.7 %collective-permute-start.2 = (bf16[64,4096]{1,0:T(8,128)(2,1)S(1)}, bf16[64,4096]{1,0:T(8,128)(2,1)S(1)}, u32[]{:S(2)}, u32[]{:S(2)}) collective-permute-start(bf16[64,4096]{1,0:T(8,128)(2,1)S(1)} %get-tuple-element.25.refs_1_), channel_id=1, source_target_pairs={{8,0},{9,1},{10,2},{11,3},{12,4},{13,5},{15,7},{16,8},{17,9},{18,1... | collective-permute-start | bytes 1572872 | tf_op jit(solution)/shard_map/ppermute | solution.py:414
  16.8 17.5 %collective-permute-start.3 = (bf16[64,4096]{1,0:T(8,128)(2,1)S(1)}, bf16[64,4096]{1,0:T(8,128)(2,1)S(1)}, u32[]{:S(2)}, u32[]{:S(2)}) collective-permute-start(bf16[64,4096]{1,0:T(8,128)(2,1)S(1)} %get-tuple-element.31), channel_id=1, source_target_pairs={{2,0},{3,1},{1,2},{8,3},{6,4},{7,5},{5,6},{12,7},{10,8},{11,9},{9,... | collective-permute-start | bytes 1572872 | tf_op jit(solution)/shard_map/ppermute | solution.py:414
  21.4 16.9 %collective-permute-start.1 = (bf16[64,4096]{1,0:T(8,128)(2,1)S(1)}, bf16[64,4096]{1,0:T(8,128)(2,1)S(1)}, u32[]{:S(2)}, u32[]{:S(2)}) collective-permute-start(bf16[64,4096]{1,0:T(8,128)(2,1)S(1)} %get-tuple-element.32), channel_id=1, source_target_pairs={{4,0},{5,1},{6,2},{7,3},{0,4},{9,5},{2,6},{11,7},{12,8},{13,9},{14... | collective-permute-start | bytes 1572872 | tf_op jit(solution)/shard_map/ppermute | solution.py:414
  34.5 11.4 %collective-permute-start.4 = (bf16[64,4096]{1,0:T(8,128)(2,1)S(1)}, bf16[64,4096]{1,0:T(8,128)(2,1)S(1)}, u32[]{:S(2)}, u32[]{:S(2)}) collective-permute-start(bf16[64,4096]{1,0:T(8,128)(2,1)S(1)} %get-tuple-element.29), channel_id=1, source_target_pairs={{2,0},{3,1},{1,2},{8,3},{6,4},{7,5},{5,6},{12,7},{10,8},{11,9},{9,... | collective-permute-start | bytes 1572872 | tf_op jit(solution)/shard_map/ppermute | solution.py:414
  36.4 17.5 %collective-permute-start.6 = (bf16[64,4096]{1,0:T(8,128)(2,1)S(1)}, bf16[64,4096]{1,0:T(8,128)(2,1)S(1)}, u32[]{:S(2)}, u32[]{:S(2)}) collective-permute-start(bf16[64,4096]{1,0:T(8,128)(2,1)S(1)} %get-tuple-element.28), channel_id=1, source_target_pairs={{4,0},{5,1},{6,2},{7,3},{0,4},{9,5},{2,6},{11,7},{12,8},{13,9},{14... | collective-permute-start | bytes 1572872 | tf_op jit(solution)/shard_map/ppermute | solution.py:414
  45.9 9.3 %collective-permute-start.5 = (bf16[64,4096]{1,0:T(8,128)(2,1)S(1)}, bf16[64,4096]{1,0:T(8,128)(2,1)S(1)}, u32[]{:S(2)}, u32[]{:S(2)}) collective-permute-start(bf16[64,4096]{1,0:T(8,128)(2,1)S(1)} %collective-permute-done.1.refs_0_), channel_id=1, source_target_pairs={{2,0},{3,1},{0,2},{1,3},{6,4},{7,5},{4,6},{5,7},{10,8},{11,9},{8,1... | collective-permute-start | bytes 1572872 | tf_op jit(solution)/shard_map/ppermute | solution.py:414
  45.9 10.1 %copy-start = (bf16[128,256]{1,0:T(8,128)(2,1)S(1)}, bf16[128,256]{1,0:T(8,128)(2,1)}, u32[]{:S(2)}) copy-start(bf16[128,256]{1,0:T(8,128)(2,1)} %constant.70.clone.refs_9_) | copy-start | bytes 196612
  53.9 2.1 %collective-permute-start.7 = (bf16[64,4096]{1,0:T(8,128)(2,1)S(1)}, bf16[64,4096]{1,0:T(8,128)(2,1)S(1)}, u32[]{:S(2)}, u32[]{:S(2)}) collective-permute-start(bf16[64,4096]{1,0:T(8,128)(2,1)S(1)} %collective-permute-done.6.refs_2_), channel_id=1, source_target_pairs={{2,0},{3,1},{0,2},{1,3},{6,4},{7,5},{4,6},{5,7},{10,8},{11,9},{8,1... | collective-permute-start | bytes 1572872 | tf_op jit(solution)/shard_map/ppermute | solution.py:414

commit v3 on v0

--- a/solution.py
+++ b/solution.py
@@ -426,10 +426,15 @@
         [table_shapes[2], pltpu.VMEM((width * (windows * depth + 1), lanes), f32), pltpu.VMEM(own_shape, bf16),
          dma((4,)), dma((4,))], work // 2,
     )
+    slots = jnp.stack([0, 1 + 2 * core, 2, 3 - 2 * core]).astype(jnp.int32)
+    offset_ids = place * owned + slots
+    keep = jnp.where(offset_ids < reach[0], jnp.float32(scale), jnp.float32(0.0))
     here, beside, across = [], [], []
     for w in range(windows):
         if w:
-            upper[w], beside[w - 1], own = lax.optimization_barrier((upper[w], beside[w - 1], own))
+            upper[w], beside[w - 1], own, slots, keep = lax.optimization_barrier(
+                (upper[w], beside[w - 1], own, slots, keep)
+            )
         for known, new in zip((here, beside, across), from_neighbours(masked[w], upper[w])):
             known.append(new)
     across[0], beside[-1] = lax.optimization_barrier((across[0], beside[-1]))
@@ -443,9 +448,6 @@
     across[-1], first = lax.optimization_barrier((across[-1], first))
     across_beside = [send(block, lambda q, p, c, g: (q, p, 1 - c, g)) for block in across]
     early = [first]
-    slots = jnp.stack([0, 1 + 2 * core, 2, 3 - 2 * core]).astype(jnp.int32)
-    offset_ids = place * owned + slots
-    keep = jnp.where(offset_ids < reach[0], jnp.float32(scale), jnp.float32(0.0))
     result = call(
         functools.partial(last_kernel, windows, len(early)), "second_pair",
         [r for both in zip(across, across_beside) for r in both],

time: 72.6 us -> 73.7 us (1.015)
  other arithmetic: 2.29 us -> 5.53 us
  waiting for transfers between devices: 17.8 us -> 15.3 us
    select_n x2, other arithmetic: 0.21 us -> 3.46 us  [from_neighbours(): return (jnp.where(place == 0, mine, upper), beside, across)]
    ppermute x8, waiting for transfers between devices: 17.8 us -> 15.3 us  [send(): return lax.ppermute(payload, ('fibre', 'freq'), pairs)]
  transfers between devices with their start and end apart: 8 -> 8, of which waited for: 4 -> 5; matrix products, arithmetic and copies ran while one was open for 0% -> 5% of each run, Pallas kernels for 26% -> 26%
where the time goes in v3:
time: 73.7 us; the launch traced here: 73.3 us
  Pallas kernels  35.2 us (48%)
  starting transfers between devices  16.5 us (22%)
  waiting for transfers between devices  15.3 us (21%)
  other arithmetic  5.53 us (8%)
  between operations  0.81 us (1%)
    pallas_call x4, Pallas kernels, call(): pl.pallas_call(kernel, out_shape=out_shape, in_specs=[vmem_spec] * len(op...  35.2 us
    ppermute x8, starting transfers between devices, send(): return lax.ppermute(payload, ('fibre', 'freq'), pairs)  16.5 us
    ppermute x8, waiting for transfers between devices, send(): return lax.ppermute(payload, ('fibre', 'freq'), pairs)  15.3 us
    select_n x2, other arithmetic, from_neighbours(): return (jnp.where(place == 0, mine, upper), beside, across)  3.46 us
  transfers between devices with their start and end apart: 8, of which 5 were waited for; matrix products, arithmetic and copies ran while one was open for 5% of the time, Pallas kernels for 26%

profile of v3, /device:TPU:21, one launch (start us, length us, event | category | flops | bytes accessed | tf_op | source)
XLA Modules:
  0.0 73.3 jit_solution(1796866820920498661)
XLA Ops:
  0.0 0.7 broadcast_compare_fusion
  0.7 1.3 %bitcast_select_fusion = (bf16[64,4096]{1,0:T(8,128)(2,1)S(1)}, bf16[64,4096]{1,0:T(8,128)(2,1)S(1)}) fusion(bf16[2,64,4096]{2,1,0:T(8,128)(2,1)} %param.8, pred[64]{0:T(512)(128)(4,1)S(1)} %broadcast_compare_fusion), kind=kLoop, calls=%fused_computation | loop fusion | flops 524288 | bytes 2097216 | tf_op jit(solution)/shard_map/jit(_where)/select_n | solution.py:372
  2.0 2.1 %collective-permute-start = (bf16[64,4096]{1,0:T(8,128)(2,1)S(1)}, bf16[64,4096]{1,0:T(8,128)(2,1)}, u32[]{:S(2)}, u32[]{:S(2)}) collective-permute-start(bf16[64,4096]{1,0:T(8,128)(2,1)S(1)} %get-tuple-element.30.refs_0_), channel_id=1, source_target_pairs={{8,0},{9,1},{10,2},{11,3},{12,4},{13,5},{15,7},{16,8},{17,9},{18,1... | collective-permute-start | bytes 1572872 | tf_op jit(solution)/shard_map/ppermute | solution.py:391
  4.1 2.1 %collective-permute-start.2 = (bf16[64,4096]{1,0:T(8,128)(2,1)S(1)}, bf16[64,4096]{1,0:T(8,128)(2,1)}, u32[]{:S(2)}, u32[]{:S(2)}) collective-permute-start(bf16[64,4096]{1,0:T(8,128)(2,1)S(1)} %get-tuple-element.29.refs_1_), channel_id=1, source_target_pairs={{8,0},{9,1},{10,2},{11,3},{12,4},{13,5},{15,7},{16,8},{17,9},{18,1... | collective-permute-start | bytes 1572872 | tf_op jit(solution)/shard_map/ppermute | solution.py:391
  6.2 4.5 %own_spectra.1.white_ref = bf16[16,256,256]{2,1,0:T(8,128)(2,1)S(1)} custom-call(bf16[64,4096]{1,0:T(8,128)(2,1)S(1)} %get-tuple-element.30.refs_0_, bf16[64,4096]{1,0:T(8,128)(2,1)S(1)} %get-tuple-element.29.refs_1_, bf16[16,256,256]{2,1,0:T(8,128)(2,1)} %constant.66.clone.refs_2_.refs_4_, bf16[16,256,256]{2,1,0:T(8,128)(2,1)} %constant.67.clone.refs_3_.refs_5_), custom_call_target="tpu_custom_call" | custom-call | flops 2147483648 | bytes 14680064 | tf_op jit(solution)/shard_map/own_spectra/pallas_call | solution.py:350
  10.8 6.0 %collective-permute-done = bf16[64,4096]{1,0:T(8,128)(2,1)} collective-permute-done((bf16[64,4096]{1,0:T(8,128)(2,1)S(1)}, bf16[64,4096]{1,0:T(8,128)(2,1)}, u32[]{:S(2)}, u32[]{:S(2)}) %collective-permute-start) | collective-permute-done | bytes 524320 | tf_op jit(solution)/shard_map/ppermute | solution.py:391
  16.8 2.3 %broadcast_select_fusion.1 = (bf16[64,4096]{1,0:T(8,128)(2,1)}, bf16[64,4096]{1,0:T(8,128)(2,1)}, bf16[64,4096]{1,0:T(8,128)(2,1)}) fusion(bf16[64,4096]{1,0:T(8,128)(2,1)S(1)} %get-tuple-element.30.refs_0_, bf16[64,4096]{1,0:T(8,128)(2,1)} %collective-permute-done, pred[]{:T(512)S(6)} %eq.10, pred[]{:T(512)S(6)} %and.28, pred[]{:T(512)S(6)} %and.26), kind=kLoop, calls=%fused_computation.3 | loop fusion | flops 786432 | bytes 2621443 | tf_op jit(solution)/shard_map/jit(_where)/select_n | solution.py:398
  19.1 4.6 %collective-permute-start.3 = (bf16[64,4096]{1,0:T(8,128)(2,1)}, bf16[64,4096]{1,0:T(8,128)(2,1)S(1)}, u32[]{:S(2)}, u32[]{:S(2)}) collective-permute-start(bf16[64,4096]{1,0:T(8,128)(2,1)} %get-tuple-element.35), channel_id=1, source_target_pairs={{2,0},{3,1},{1,2},{8,3},{6,4},{7,5},{5,6},{12,7},{10,8},{11,9},{9,... | collective-permute-start | bytes 1572872 | tf_op jit(solution)/shard_map/ppermute | solution.py:391
  24.4 0.1 compare_select_fusion
  24.4 0.0 copy-start
  24.4 3.1 %collective-permute-start.1 = (bf16[64,4096]{1,0:T(8,128)(2,1)}, bf16[64,4096]{1,0:T(8,128)(2,1)S(1)}, u32[]{:S(2)}, u32[]{:S(2)}) collective-permute-start(bf16[64,4096]{1,0:T(8,128)(2,1)} %get-tuple-element.36), channel_id=1, source_target_pairs={{4,0},{5,1},{6,2},{7,3},{0,4},{9,5},{2,6},{11,7},{12,8},{13,9},{14... | collective-permute-start | bytes 1572872 | tf_op jit(solution)/shard_map/ppermute | solution.py:391
  27.6 6.4 %own_bins.1.refs_7_ = bf16[128,128,128]{2,1,0:T(8,128)(2,1)} custom-call(bf16[16,256,256]{2,1,0:T(8,128)(2,1)S(1)} %own_spectra.1.white_ref, bf16[16,512,256]{2,1,0:T(8,128)(2,1)} %constant.68.clone.bins_hbm), custom_call_target="tpu_custom_call" | custom-call | flops 2147483648 | bytes 14680064 | tf_op jit(solution)/shard_map/own_bins/pallas_call | solution.py:350
  34.0 0.0 collective-permute-done.2
  34.0 0.4 collective-permute-done.3.refs_1_
  34.3 1.1 %broadcast_select_fusion = (bf16[64,4096]{1,0:T(8,128)(2,1)S(1)}, bf16[64,4096]{1,0:T(8,128)(2,1)S(1)}, bf16[64,4096]{1,0:T(8,128)(2,1)S(1)}) fusion(bf16[64,4096]{1,0:T(8,128)(2,1)S(1)} %get-tuple-element.29.refs_1_, bf16[64,4096]{1,0:T(8,128)(2,1)} %collective-permute-done.2, pred[]{:T(512)S(6)} %eq.10, pred[]{:T(512)S(6)} %and.26, pred[]{:T(512)S(6)} %and.28), kind=kLoop, calls=%fused_computation.2 | loop fusion | flops 786432 | bytes 2621443 | tf_op jit(solution)/shard_map/jit(_where)/select_n | solution.py:398
  35.5 1.9 %collective-permute-start.4 = (bf16[64,4096]{1,0:T(8,128)(2,1)S(1)}, bf16[64,4096]{1,0:T(8,128)(2,1)S(1)}, u32[]{:S(2)}, u32[]{:S(2)}) collective-permute-start(bf16[64,4096]{1,0:T(8,128)(2,1)S(1)} %get-tuple-element.33), channel_id=1, source_target_pairs={{2,0},{3,1},{1,2},{8,3},{6,4},{7,5},{5,6},{12,7},{10,8},{11,9},{9,... | collective-permute-start | bytes 1572872 | tf_op jit(solution)/shard_map/ppermute | solution.py:391
  37.4 2.1 %collective-permute-start.6 = (bf16[64,4096]{1,0:T(8,128)(2,1)S(1)}, bf16[64,4096]{1,0:T(8,128)(2,1)S(1)}, u32[]{:S(2)}, u32[]{:S(2)}) collective-permute-start(bf16[64,4096]{1,0:T(8,128)(2,1)S(1)} %get-tuple-element.32), channel_id=1, source_target_pairs={{4,0},{5,1},{6,2},{7,3},{0,4},{9,5},{2,6},{11,7},{12,8},{13,9},{14... | collective-permute-start | bytes 1572872 | tf_op jit(solution)/shard_map/ppermute | solution.py:391
  39.5 0.7 collective-permute-done.1.refs_0_
  40.2 6.7 %collective-permute-done.4.refs_3_ = bf16[64,4096]{1,0:T(8,128)(2,1)S(1)} collective-permute-done((bf16[64,4096]{1,0:T(8,128)(2,1)S(1)}, bf16[64,4096]{1,0:T(8,128)(2,1)S(1)}, u32[]{:S(2)}, u32[]{:S(2)}) %collective-permute-start.4) | collective-permute-done | bytes 524320 | tf_op jit(solution)/shard_map/ppermute | solution.py:391
  46.9 0.0 collective-permute-start.5
  46.9 0.0 copy-done
  46.9 0.0 copy-start.1
  46.9 7.9 %first_pair.1.refs_8_ = bf16[128,128,128]{2,1,0:T(8,128)(2,1)} custom-call(bf16[64,4096]{1,0:T(8,128)(2,1)S(1)} %copy-done, bf16[64,4096]{1,0:T(8,128)(2,1)S(1)} %collective-permute-done.3.refs_1_, bf16[64,4096]{1,0:T(8,128)(2,1)S(1)} %get-tuple-element.31.refs_2_, bf16[64,4096]{1,0:T(8,128)(2,1)S(1)} %collective-permute-done.4.refs_3_, ...), custom_call_target="tpu_custom_call" | custom-call | flops 4294967296 | bytes 14680064 | tf_op jit(solution)/shard_map/first_pair/pallas_call | solution.py:350
  54.8 0.0 collective-permute-done.6.refs_2_
  54.8 0.6 collective-permute-start.7
  55.4 0.0 collective-permute-done.5.refs_1_
  55.4 1.5 %collective-permute-done.7.refs_3_ = bf16[64,4096]{1,0:T(8,128)(2,1)S(1)} collective-permute-done((bf16[64,4096]{1,0:T(8,128)(2,1)S(1)}, bf16[64,4096]{1,0:T(8,128)(2,1)S(1)}, u32[]{:S(2)}, u32[]{:S(2)}) %collective-permute-start.7) | collective-permute-done | bytes 524320 | tf_op jit(solution)/shard_map/ppermute | solution.py:391
  56.9 0.0 copy-done.1
  56.9 16.4 %second_pair.1 = f32[4,64,64,128]{3,2,1,0:T(8,128)} custom-call(bf16[64,4096]{1,0:T(8,128)(2,1)S(1)} %collective-permute-done.1.refs_0_, bf16[64,4096]{1,0:T(8,128)(2,1)S(1)} %collective-permute-done.5.refs_1_, bf16[64,4096]{1,0:T(8,128)(2,1)S(1)} %collective-permute-done.6.refs_2_, bf16[64,4096]{1,0:T(8,128)(2,1)S(1)} %collective-permute-done.7.refs_3_, ...), custom_call_target="tpu_custom_call" | custom-call | flops 8589934592 | bytes 14680064 | tf_op jit(solution)/shard_map/second_pair/pallas_call | solution.py:350
Async XLA Ops:
  2.0 14.8 %collective-permute-start = (bf16[64,4096]{1,0:T(8,128)(2,1)S(1)}, bf16[64,4096]{1,0:T(8,128)(2,1)}, u32[]{:S(2)}, u32[]{:S(2)}) collective-permute-start(bf16[64,4096]{1,0:T(8,128)(2,1)S(1)} %get-tuple-element.30.refs_0_), channel_id=1, source_target_pairs={{8,0},{9,1},{10,2},{11,3},{12,4},{13,5},{15,7},{16,8},{17,9},{18,1... | collective-permute-start | bytes 1572872 | tf_op jit(solution)/shard_map/ppermute | solution.py:391
  4.1 29.9 %collective-permute-start.2 = (bf16[64,4096]{1,0:T(8,128)(2,1)S(1)}, bf16[64,4096]{1,0:T(8,128)(2,1)}, u32[]{:S(2)}, u32[]{:S(2)}) collective-permute-start(bf16[64,4096]{1,0:T(8,128)(2,1)S(1)} %get-tuple-element.29.refs_1_), channel_id=1, source_target_pairs={{8,0},{9,1},{10,2},{11,3},{12,4},{13,5},{15,7},{16,8},{17,9},{18,1... | collective-permute-start | bytes 1572872 | tf_op jit(solution)/shard_map/ppermute | solution.py:391
  19.1 15.2 %collective-permute-start.3 = (bf16[64,4096]{1,0:T(8,128)(2,1)}, bf16[64,4096]{1,0:T(8,128)(2,1)S(1)}, u32[]{:S(2)}, u32[]{:S(2)}) collective-permute-start(bf16[64,4096]{1,0:T(8,128)(2,1)} %get-tuple-element.35), channel_id=1, source_target_pairs={{2,0},{3,1},{1,2},{8,3},{6,4},{7,5},{5,6},{12,7},{10,8},{11,9},{9,... | collective-permute-start | bytes 1572872 | tf_op jit(solution)/shard_map/ppermute | solution.py:391
  24.4 22.5 %copy-start = (bf16[64,4096]{1,0:T(8,128)(2,1)S(1)}, bf16[64,4096]{1,0:T(8,128)(2,1)}, u32[]{:S(2)}) copy-start(bf16[64,4096]{1,0:T(8,128)(2,1)} %get-tuple-element.34.refs_0_) | copy-start | bytes 1572868
  24.4 15.8 %collective-permute-start.1 = (bf16[64,4096]{1,0:T(8,128)(2,1)}, bf16[64,4096]{1,0:T(8,128)(2,1)S(1)}, u32[]{:S(2)}, u32[]{:S(2)}) collective-permute-start(bf16[64,4096]{1,0:T(8,128)(2,1)} %get-tuple-element.36), channel_id=1, source_target_pairs={{4,0},{5,1},{6,2},{7,3},{0,4},{9,5},{2,6},{11,7},{12,8},{13,9},{14... | collective-permute-start | bytes 1572872 | tf_op jit(solution)/shard_map/ppermute | solution.py:391
  35.5 11.4 %collective-permute-start.4 = (bf16[64,4096]{1,0:T(8,128)(2,1)S(1)}, bf16[64,4096]{1,0:T(8,128)(2,1)S(1)}, u32[]{:S(2)}, u32[]{:S(2)}) collective-permute-start(bf16[64,4096]{1,0:T(8,128)(2,1)S(1)} %get-tuple-element.33), channel_id=1, source_target_pairs={{2,0},{3,1},{1,2},{8,3},{6,4},{7,5},{5,6},{12,7},{10,8},{11,9},{9,... | collective-permute-start | bytes 1572872 | tf_op jit(solution)/shard_map/ppermute | solution.py:391
  37.4 17.4 %collective-permute-start.6 = (bf16[64,4096]{1,0:T(8,128)(2,1)S(1)}, bf16[64,4096]{1,0:T(8,128)(2,1)S(1)}, u32[]{:S(2)}, u32[]{:S(2)}) collective-permute-start(bf16[64,4096]{1,0:T(8,128)(2,1)S(1)} %get-tuple-element.32), channel_id=1, source_target_pairs={{4,0},{5,1},{6,2},{7,3},{0,4},{9,5},{2,6},{11,7},{12,8},{13,9},{14... | collective-permute-start | bytes 1572872 | tf_op jit(solution)/shard_map/ppermute | solution.py:391
  46.9 8.5 %collective-permute-start.5 = (bf16[64,4096]{1,0:T(8,128)(2,1)S(1)}, bf16[64,4096]{1,0:T(8,128)(2,1)S(1)}, u32[]{:S(2)}, u32[]{:S(2)}) collective-permute-start(bf16[64,4096]{1,0:T(8,128)(2,1)S(1)} %collective-permute-done.1.refs_0_), channel_id=1, source_target_pairs={{2,0},{3,1},{0,2},{1,3},{6,4},{7,5},{4,6},{5,7},{10,8},{11,9},{8,1... | collective-permute-start | bytes 1572872 | tf_op jit(solution)/shard_map/ppermute | solution.py:391
  46.9 10.0 %copy-start.1 = (bf16[128,256]{1,0:T(8,128)(2,1)S(1)}, bf16[128,256]{1,0:T(8,128)(2,1)}, u32[]{:S(2)}) copy-start(bf16[128,256]{1,0:T(8,128)(2,1)} %constant.70.clone.refs_9_) | copy-start | bytes 196612
  54.8 2.1 %collective-permute-start.7 = (bf16[64,4096]{1,0:T(8,128)(2,1)S(1)}, bf16[64,4096]{1,0:T(8,128)(2,1)S(1)}, u32[]{:S(2)}, u32[]{:S(2)}) collective-permute-start(bf16[64,4096]{1,0:T(8,128)(2,1)S(1)} %collective-permute-done.6.refs_2_), channel_id=1, source_target_pairs={{2,0},{3,1},{0,2},{1,3},{6,4},{7,5},{4,6},{5,7},{10,8},{11,9},{8,1... | collective-permute-start | bytes 1572872 | tf_op jit(solution)/shard_map/ppermute | solution.py:391
